TPU v7x, 32 devices: a whole 2x2x4 slice. The times are simulated.
32 devices in a mesh: ens: 8 (over z, core), pen: 4 (over y, x).
Axes of the slice: x: 2, y: 2, z: 4, core: 2. Of those that a mesh axis runs over, the one named last changes fastest.
Arguments:
- state: float32 [2, 8, 4, 256, 512], P(None, 'ens', None, 'pen'), may hold values from -8 to 8, as said below
- accum: float32 [2, 8, 4, 256, 512], P(None, 'ens', None, 'pen'), may hold values from -8 to 8, as said below
- base_flow: float32 [6, 4, 256, 256], P(None, None, 'pen', 'ens'), may hold values from -6 to 6
Outputs:
- state_next: float32 [2, 8, 4, 256, 512], P(None, 'ens', None, 'pen')
- accum_next: float32 [2, 8, 4, 256, 512], P(None, 'ens', None, 'pen')
Inputs may be any that keep to these rules, and one draw needn't show every extreme that they name: `state`: each field of each perturbation and level is the spectrum of a real field: the entry at ((256 - ky) mod 256, (256 - kx) mod 256) is the complex conjugate of the entry at (ky, kx). `accum`: each field of each perturbation and level is the spectrum of a real field: the entry at ((256 - ky) mod 256, (256 - kx) mod 256) is the complex conjugate of the entry at (ky, kx).
All inputs are finite; a program needn't handle non-finite values.
Results may differ from a plain program's by a relative error of at most 0.0003.
Values sent between devices are 32-bit elements; how exact they have to be, the bound alone decides.
No kernel may reach another device: no remote copies, remote signals or barrier semaphores. Data moves between devices by JAX's collectives and lax.ppermute only.
A program may use at most 64 MiB of HBM per device.

v0:
```python
import functools
import math

import jax
import jax.numpy as jnp
import ml_dtypes
import numpy as np
from jax import lax
from jax.experimental import pallas as pl
from jax.experimental.pallas import tpu as pltpu
from jax.sharding import PartitionSpec as P

viscosity = 0.05
diffusivity = 0.05
vertical_mixing = 0.5
buoyancy_gain = 0.5
stratification = 0.5
memory_factor = -5.0 / 9.0
weight_factor = 15.0 / 16.0
time_step = 0.4


def wave_numbers(amount, offset, length):
    position = offset + jnp.arange(amount, dtype=jnp.int32)
    half_length = length // 2
    signed = jnp.where(position <= half_length, position, position - length)
    derivative = jnp.where(position == half_length, 0, signed)
    return (2.0 * math.pi / length * derivative.astype(jnp.float32), signed)


def times_i(real_part, imag_part, factor):
    return (-factor * imag_part, factor * real_part)


def vertical(quantity, level_axis):
    depth = quantity.shape[level_axis]
    lower = lax.slice_in_dim(quantity, 0, 1, axis=level_axis)
    upper = lax.slice_in_dim(quantity, depth - 1, depth, axis=level_axis)
    padded = jnp.concatenate([lower, quantity, upper], axis=level_axis)
    above = lax.slice_in_dim(padded, 2, depth + 2, axis=level_axis)
    below = lax.slice_in_dim(padded, 0, depth, axis=level_axis)
    return above + below - 2.0 * quantity


def tendency(vort, buoy, advect, across, kappa_x, square, level_axis):
    tend_vort_re = (
        -advect[0]
        + buoyancy_gain * (-kappa_x * buoy[1])
        - viscosity * square * vort[0]
        + vertical_mixing * vertical(vort[0], level_axis)
    )
    tend_vort_im = (
        -advect[1]
        + buoyancy_gain * (kappa_x * buoy[0])
        - viscosity * square * vort[1]
        + vertical_mixing * vertical(vort[1], level_axis)
    )
    tend_buoy_re = (
        -advect[2]
        - stratification * across[0]
        - diffusivity * square * buoy[0]
        + vertical_mixing * vertical(buoy[0], level_axis)
    )
    tend_buoy_im = (
        -advect[3]
        - stratification * across[1]
        - diffusivity * square * buoy[1]
        + vertical_mixing * vertical(buoy[1], level_axis)
    )
    return jnp.stack(
        [
            jnp.concatenate([tend_vort_re, tend_vort_im], axis=-1),
            jnp.concatenate([tend_buoy_re, tend_buoy_im], axis=-1),
        ]
    )


def dft_tables(length):
    position = jnp.arange(length, dtype=jnp.int32)
    product = position[:, None] * position[None, :] % length
    angle = 2.0 * math.pi / length * product.astype(jnp.float32)
    scale = 1.0 / math.sqrt(length)
    return (scale * jnp.cos(angle), scale * jnp.sin(angle))


def to_physical(spectral, x_table, y_table):
    mixed_space = jnp.einsum(
        "fplkj,jcx->fplcxk", spectral, x_table, precision=lax.Precision.HIGHEST
    )
    return jnp.einsum(
        "fplcxk,ckm->fplxm",
        lax.all_to_all(mixed_space, "pen", split_axis=4, concat_axis=5, tiled=True),
        y_table,
        precision=lax.Precision.HIGHEST,
    )


def on_device_general(state, accum, base_flow):
    grid_size = state.shape[-1] // 2
    row_count = state.shape[3]
    base_all = lax.all_gather(base_flow, "ens", axis=3, tiled=True)
    kappa_rows, signed_y = wave_numbers(row_count, lax.axis_index("pen") * row_count, grid_size)
    kappa_cols, signed_x = wave_numbers(grid_size, 0, grid_size)
    kappa_y = kappa_rows[:, None]
    kappa_x = kappa_cols[None, :]
    wave_square = signed_y[:, None] ** 2 + signed_x[None, :] ** 2
    factor = (2.0 * math.pi / grid_size) ** 2
    square = factor * wave_square.astype(jnp.float32)
    inverse = jnp.where(
        wave_square > 0, 1.0 / (factor * jnp.maximum(wave_square, 1).astype(jnp.float32)), 0.0
    )
    vort = (state[0][..., :grid_size], state[0][..., grid_size:])
    buoy = (state[1][..., :grid_size], state[1][..., grid_size:])
    potential_re = -vort[0] * inverse
    potential_im = -vort[1] * inverse
    flow_x = times_i(potential_re, potential_im, -kappa_y)
    flow_y = times_i(potential_re, potential_im, kappa_x)
    vort_x = times_i(vort[0], vort[1], kappa_x)
    vort_y = times_i(vort[0], vort[1], kappa_y)
    buoy_x = times_i(buoy[0], buoy[1], kappa_x)
    buoy_y = times_i(buoy[0], buoy[1], kappa_y)
    cosine_table, sine_table = dft_tables(grid_size)
    x_table = jnp.concatenate(
        [
            jnp.stack([cosine_table, sine_table], axis=1),
            jnp.stack([-sine_table, cosine_table], axis=1),
        ],
        axis=0,
    )
    y_table = jnp.stack([cosine_table, -sine_table])
    components = [flow_x, flow_y, vort_x, vort_y, buoy_x, buoy_y]
    spectral = jnp.stack([jnp.concatenate(component, axis=-1) for component in components])
    physical = to_physical(spectral, x_table, y_table)
    flow_x_p, flow_y_p = (physical[0], physical[1])
    vort_x_p, vort_y_p = (physical[2], physical[3])
    buoy_x_p, buoy_y_p = (physical[4], physical[5])
    advect_vort = (
        base_all[0] * vort_x_p
        + base_all[1] * vort_y_p
        + flow_x_p * base_all[2]
        + flow_y_p * base_all[3]
    )
    advect_buoy = (
        base_all[0] * buoy_x_p
        + base_all[1] * buoy_y_p
        + flow_x_p * base_all[4]
        + flow_y_p * base_all[5]
    )
    advect_both = jnp.stack([advect_vort, advect_buoy])
    y_forward = jnp.stack([cosine_table, -sine_table], axis=1)
    x_forward = jnp.stack(
        [
            jnp.concatenate([cosine_table, -sine_table], axis=1),
            jnp.concatenate([sine_table, cosine_table], axis=1),
        ]
    )
    spread = jnp.einsum(
        "fplxy,yck->fplckx", advect_both, y_forward, precision=lax.Precision.HIGHEST
    )
    spectra = jnp.einsum(
        "fplckx,cxm->fplkm",
        lax.all_to_all(spread, "pen", split_axis=4, concat_axis=5, tiled=True),
        x_forward,
        precision=lax.Precision.HIGHEST,
    )
    advect = (
        spectra[0][..., :grid_size],
        spectra[0][..., grid_size:],
        spectra[1][..., :grid_size],
        spectra[1][..., grid_size:],
    )
    tend = tendency(vort, buoy, advect, flow_y, kappa_x, square, 1)
    accum_next = memory_factor * accum + tend
    state_next = state + weight_factor * time_step * accum_next
    return (state_next, accum_next)


PEN = 4
EXTRA = 8
HINT = dict(own=0, inverse=10**10, forward=10**10, pack=0, advect=(0, 0), final=0)


def split(values):
    high = values.astype(jnp.bfloat16)
    return high, (values - high.astype(jnp.float32)).astype(jnp.bfloat16)


def split_table(values):
    high = values.astype(ml_dtypes.bfloat16)
    low = (values - high.astype(np.float64)).astype(ml_dtypes.bfloat16)
    return np.stack([high, low], axis=-3)


def cosine(grid, left, right):
    return np.cos(2.0 * np.pi / grid * (left * right % grid)) / math.sqrt(grid)


def sine(grid, left, right):
    return np.sin(2.0 * np.pi / grid * (left * right % grid)) / math.sqrt(grid)


def x_table(grid):
    kx = np.arange(grid)
    x = kx[:, None]
    return split_table(np.concatenate([cosine(grid, x, kx), sine(grid, x, kx)], axis=1))


def y_inverse_table(grid):
    rows = grid // PEN
    y = np.arange(grid)[:, None]
    tables = []
    for device in range(PEN):
        ky = np.concatenate([block * rows + np.arange(rows) for block in (device, device ^ 2)])
        real = np.where(ky % (grid // 2) == 0, 1.0, 2.0) * cosine(grid, y, ky)
        imag = -2.0 * sine(grid, y, ky)
        near, far = (device ^ 1) * rows, (device ^ 3) * rows
        if device % 2 == 0:
            imag[:, 0] = 2.0 * cosine(grid, y[:, 0], near)
            imag[:, rows] = -2.0 * sine(grid, y[:, 0], near)
        else:
            real[:, rows] = cosine(grid, y[:, 0], near)
            imag[:, rows] = cosine(grid, y[:, 0], far)
        tables.append(np.concatenate([real, imag], axis=1))
    return split_table(np.stack(tables))


def y_forward_table(grid):
    rows = grid // PEN
    parts = []
    for device in range(PEN):
        ky = device * rows + np.arange(rows)[:, None]
        y = np.arange(grid)[None, :]
        parts += [cosine(grid, ky, y), -sine(grid, ky, y)]
    return split_table(np.concatenate([np.concatenate(parts[:4]), np.concatenate(parts[4:])], axis=1))


def dot(left, right):
    return jnp.dot(left, right, preferred_element_type=jnp.float32)


def dot_split(left, right):
    return dot(left[0], right[0]) + (dot(left[1], right[0]) + dot(left[0], right[1]))


def waves(position, grid):
    signed = jnp.where(position <= grid // 2, position, position - grid)
    derivative = jnp.where(position == grid // 2, 0, signed)
    return (2.0 * math.pi / grid) * derivative.astype(jnp.float32), signed


def wave_arrays(row_position, grid):
    kappa_y, signed_y = waves(row_position, grid)
    kappa_x, signed_x = waves(lax.broadcasted_iota(jnp.int32, (1, grid), 1), grid)
    wave_square = signed_y * signed_y + signed_x * signed_x
    factor = (2.0 * math.pi / grid) ** 2
    square = factor * wave_square.astype(jnp.float32)
    inverse = jnp.where(wave_square > 0, 1.0 / jnp.where(wave_square > 0, square, 1.0), 0.0)
    return kappa_y, kappa_x, square, inverse


def interleave(even, odd):
    low_lanes = lax.broadcasted_iota(jnp.int32, (1, 128), 1) < 64
    return (
        jnp.where(low_lanes, even, pltpu.roll(odd, 64, 1)),
        jnp.where(low_lanes, pltpu.roll(even, 64, 1), odd),
    )


def base_kernel(base_ref, own_ref, swap_ref):
    mine = (lax.axis_index("pen") % 2) * 2
    for out_ref, first in ((own_ref, mine), (swap_ref, 2 - mine)):
        for field in range(base_ref.shape[0]):
            out_ref[:, 128 * field : 128 * field + 128] = jnp.concatenate(
                [base_ref[field, first], base_ref[field, first + 1]], axis=1
            )


def near_kernel(block_ref, state_ref, swap_ref, near_ref, far_ref):
    mine = (lax.axis_index("pen") % 2) * 2
    tall = block_ref.shape[0]
    swap_ref[:tall, :] = block_ref[...]
    swap_ref[tall:, :] = jnp.zeros((EXTRA, swap_ref.shape[1]), jnp.float32)
    far_ref[...] = jnp.zeros_like(far_ref)
    for index in range(4):
        field, level = index // 2, index % 2
        line = state_ref[field, 0, 2 - mine + level, 0:1, :]
        near_ref[index] = state_ref[field, 0, mine + level]
        far_ref[index : index + 1, :] = line
        swap_ref[tall + index : tall + index + 1, : far_ref.shape[1]] = line


def x_stage(grid, table, ky, held):
    count = held[0].shape[0]
    kappa_y, kappa_x, _, inverse = wave_arrays(ky, grid)
    fields = [
        (0, inverse, kappa_y),
        (0, -kappa_x * inverse, None),
        (0, kappa_x, None),
        (0, None, kappa_y),
        (1, kappa_x, None),
        (1, None, kappa_y),
    ]
    for field, before, after in fields:
        stacked = []
        for level in range(2):
            for columns in (slice(0, grid), slice(grid, 2 * grid)):
                values = held[2 * field + level][:, columns]
                stacked.append(values if before is None else values * before)
        product = dot_split(split(jnp.concatenate(stacked, axis=0)), table)
        results = []
        for level in range(2):
            top = product[2 * level * count : (2 * level + 1) * count]
            bottom = product[(2 * level + 1) * count : (2 * level + 2) * count]
            real = -(bottom[:, :128] + top[:, 128:])
            imag = top[:, :128] - bottom[:, 128:]
            results.append((real, imag) if after is None else (after * real, after * imag))
        yield results


def x_columns(grid, x_ref):
    start = pl.multiple_of((lax.axis_index("pen") // 2) * 128, 128)
    return [
        jnp.concatenate(
            [x_ref[part, :, pl.ds(start, 128)], x_ref[part, :, pl.ds(grid + start, 128)]], axis=1
        )
        for part in range(2)
    ]


def own_rows_kernel(grid, state_ref, x_ref, real_ref, imag_ref):
    rows = state_ref.shape[3]
    pen = lax.axis_index("pen")
    mine = (pen % 2) * 2
    held = [state_ref[field, 0, mine + level] for field in range(2) for level in range(2)]
    ky = pen * rows + lax.broadcasted_iota(jnp.int32, (rows, 1), 0)
    for number, results in enumerate(x_stage(grid, x_columns(grid, x_ref), ky, held)):
        for level, (real, imag) in enumerate(results):
            real_ref[level, number] = real
            imag_ref[level, number] = imag


def inverse_kernel(
    grid, near_ref, far_ref, came_ref, own_real, own_imag, x_ref, y_ref, own_ref, swap_ref, mixed, high_ref, low_ref, y_held, sem
):
    y_copy = pltpu.make_async_copy(y_ref.at[lax.axis_index("pen")], y_held, sem)
    y_copy.start()
    rows = own_real.shape[2]
    pen = lax.axis_index("pen")
    odd = pen % 2 == 1
    count = rows + EXTRA
    tall = came_ref.shape[0] - EXTRA
    held = [
        jnp.concatenate(
            [
                near_ref[index],
                came_ref[tall + index : tall + index + 1, : 2 * grid],
                far_ref[index : index + 1, :],
                jnp.zeros((EXTRA - 2, 2 * grid), jnp.float32),
            ],
            axis=0,
        )
        for index in range(4)
    ]
    row = lax.broadcasted_iota(jnp.int32, (count, 1), 0)
    ky = jnp.where(row < rows, (pen ^ 2) * rows + row, (pen ^ 1) * rows)
    ky = jnp.where(row > rows, (pen ^ 3) * rows, ky)
    for number, results in enumerate(x_stage(grid, x_columns(grid, x_ref), ky, held)):
        for level, (real, imag) in enumerate(results):
            first_imag = own_imag[level, number, 0:1, :]
            mixed[level, :rows, :] = own_real[level, number]
            mixed[level, rows : 2 * rows, :] = real[:rows]
            mixed[level, 2 * rows : 3 * rows, :] = own_imag[level, number]
            mixed[level, 3 * rows :, :] = imag[:rows]
            near_real, near_imag = real[rows : rows + 1], imag[rows : rows + 1]
            far_real = real[rows + 1 : rows + 2]
            mixed[level, rows : rows + 1, :] = jnp.where(odd, near_real, real[0:1])
            mixed[level, 2 * rows : 2 * rows + 1, :] = jnp.where(odd, first_imag, near_real)
            mixed[level, 3 * rows : 3 * rows + 1, :] = jnp.where(odd, far_real, near_imag)
        for block, values in enumerate(interleave(mixed[0], mixed[1])):
            high, low = split(values)
            high_ref[block ^ (pen % 2), :, 128 * number : 128 * number + 128] = high
            low_ref[block ^ (pen % 2), :, 128 * number : 128 * number + 128] = low
    y_copy.wait()
    left = (y_held[0], y_held[1])
    own_ref[...] = dot_split(left, (high_ref[0], low_ref[0]))
    swap_ref[...] = dot_split(left, (high_ref[1], low_ref[1]))


def advection_kernel(places, field, own_ref, swap_ref, *refs):
    packs, (table_ref, *outs, high_ref, low_ref) = refs[:2], refs[2:]
    ens = lax.axis_index("ens")
    tall = packs[0].shape[0] // len(places)
    for which in range(2):
        for slot, (offset, chunk) in enumerate(places):
            place = pl.ds(pl.multiple_of((ens ^ offset ^ which) * tall, tall), tall)
            along_ref = (own_ref, swap_ref)[chunk]

            def base(index, which=which, slot=slot):
                return packs[which][tall * slot : tall * (slot + 1), 128 * index : 128 * index + 128]

            def along(index, place=place, along_ref=along_ref):
                return along_ref[place, 128 * index : 128 * index + 128]

            first = 2 + 2 * field
            total = (
                base(0) * along(first)
                + base(1) * along(first + 1)
                + along(0) * base(first)
                + along(1) * base(first + 1)
            )
            lanes = slice(128 * chunk, 128 * chunk + 128)
            high_ref[place, lanes], low_ref[place, lanes] = split(total)
    pen = lax.axis_index("pen")
    grid = table_ref.shape[1]
    rows = grid // PEN
    for step in range(PEN):
        target = pen ^ step
        place = pl.ds(pl.multiple_of((target % 2) * 2 * rows, 2 * rows), 2 * rows)
        lanes = pl.ds(pl.multiple_of((target // 2) * grid, grid), grid)
        outs[step][...] = dot_split(
            (table_ref[2, place, lanes], table_ref[3, place, lanes]), (high_ref[...], low_ref[...])
        )


def final_kernel(grid, field, *refs):
    messages, (state_ref, accum_ref, table_ref) = refs[:PEN], refs[PEN : PEN + 3]
    state_out, accum_out, gathered, state_next, accum_next, sems = refs[-6:]
    rows, levels = state_ref.shape[3], state_ref.shape[2]
    pen = lax.axis_index("pen")
    for step in range(PEN):
        gathered[pen ^ step] = messages[step][...]
    row = lax.broadcasted_iota(jnp.int32, (rows, 1), 0)
    _, kappa_x, square, inverse = wave_arrays(pen * rows + row, grid)
    table = (table_ref[0], table_ref[1])
    real, imag = slice(0, grid), slice(grid, 2 * grid)
    copies = []
    for pair in range(levels // 2):
        first, second = [slice(128 * chunk, 128 * chunk + 128) for chunk in (pair, 1 - pair)]
        halves = [
            interleave(gathered[pair + 2 * block, :, first], gathered[pair + 2 * block, :, second])
            for block in range(2)
        ]
        left = jnp.concatenate(
            [jnp.concatenate([half[level] for half in halves], axis=1) for level in range(2)], axis=0
        )
        product = dot_split(split(left), table)
        for level in (2 * pair, 2 * pair + 1):
            start = 2 * rows * (level - 2 * pair)
            top, bottom = product[start : start + rows], product[start + rows : start + 2 * rows]
            for columns, other, sign, advect in (
                (real, imag, 1.0, top[:, :grid] + bottom[:, grid:]),
                (imag, real, -1.0, bottom[:, :grid] - top[:, grid:]),
            ):
                here = state_ref[field, 0, level, :, columns]
                above = state_ref[field, 0, min(level + 1, levels - 1), :, columns]
                below = state_ref[field, 0, max(level - 1, 0), :, columns]
                cross = state_ref[1 - field, 0, level, :, other]
                if field == 0:
                    coupling = (-sign * buoyancy_gain) * (kappa_x * cross)
                else:
                    coupling = (-sign * stratification) * (kappa_x * inverse * cross)
                damping = viscosity if field == 0 else diffusivity
                memory = (
                    memory_factor * accum_ref[field, 0, level, :, columns]
                    - advect
                    + coupling
                    - damping * square * here
                    + vertical_mixing * (above + below - 2.0 * here)
                )
                accum_next[level, :, columns] = memory
                state_next[level, :, columns] = here + weight_factor * time_step * memory
            for which, (held, out) in enumerate(((state_next, state_out), (accum_next, accum_out))):
                copy = pltpu.make_async_copy(
                    held.at[level], out.at[field, 0, level], sems.at[which, level]
                )
                copy.start()
                copies.append(copy)
    for copy in copies:
        copy.wait()


def pack_kernel(*refs):
    start, total = 0, refs[-1].shape[0]
    for ref in refs[:-1]:
        count = min(ref.shape[0], total - start)
        refs[-1][start : start + count, :] = ref[:count, :]
        start += count


def call(kernel, outs, scratch, cost, args, after=(), into=None, outside=()):
    args, after = list(args), list(after) + list(into or ())
    count, total = len(args), len(args) + len(after)
    size = sum(math.prod(a.shape) * a.dtype.itemsize for a in args + list(outs))
    first = total - len(into or ())
    return pl.pallas_call(
        lambda *refs: kernel(*refs[:count], *refs[total:]),
        out_shape=outs,
        in_specs=[
            pl.BlockSpec(memory_space=pl.ANY if index in outside else pltpu.VMEM) for index in range(count)
        ]
        + [pl.BlockSpec(memory_space=pl.ANY)] * len(after),
        out_specs=[pl.BlockSpec(memory_space=pltpu.VMEM if into is None else pl.ANY)] * len(outs),
        scratch_shapes=scratch,
        input_output_aliases={first + index: index for index in range(total - first)},
        compiler_params=pltpu.CompilerParams(vmem_limit_bytes=24 * 1024 * 1024),
        cost_estimate=pl.CostEstimate(flops=cost, bytes_accessed=size, transcendentals=0),
        name=getattr(kernel, "func", kernel).__name__,
    )(*args, *after)


def exchange(values, axis, size, mask):
    return lax.ppermute(values, axis, [(index, index ^ mask) for index in range(size)])


def pack(arrays, cost=0, after=(), drop=0):
    total = sum(array.shape[0] for array in arrays) - drop
    shape = jax.ShapeDtypeStruct((total, arrays[0].shape[1]), arrays[0].dtype)
    return call(pack_kernel, [shape], [], cost, arrays, after=after)[0]


def on_device(axes, state, accum, base_flow):
    grid, rows, levels = state.shape[-1] // 2, state.shape[3], state.shape[2]
    size = axes["ens"]
    if axes["pen"] != PEN or levels != 4 or grid != 256 or size != 8:
        return on_device_general(state, accum, base_flow)
    f32, bf16 = jnp.float32, jnp.bfloat16
    shape = functools.partial(jax.ShapeDtypeStruct, dtype=f32)
    fields, _, wide, tall = base_flow.shape
    lanes = 2 * wide
    base_lanes = fields * lanes
    table = jnp.asarray(np.concatenate([x_table(grid), y_forward_table(grid)]))
    y_table = y_inverse_table(grid)

    def near(values, mask):
        return exchange(values, "ens", size, mask)

    def across(values, mask):
        return exchange(values, ("ens", "pen"), size * PEN, mask * PEN + 1)

    own_base, swap_base = call(
        base_kernel, [shape((tall, base_lanes))] * 2, [], 0, [jnp.swapaxes(base_flow, 2, 3)]
    )
    own_far, swap_far = near(own_base, 6), across(swap_base, 6)
    swap_message, rows_message, far_message = call(
        near_kernel,
        [shape((tall + EXTRA, base_lanes)), shape((4, rows, 2 * grid)), shape((EXTRA, 2 * grid))],
        [],
        0,
        [swap_base, state],
        after=[own_base],
    )
    near_rows = exchange(rows_message, "pen", PEN, 2)
    own_near = near(pack([own_base], after=[rows_message]), 2)
    swap_near = across(pack([swap_base], after=[rows_message]), 2)
    came = exchange(swap_message, "pen", PEN, 1)
    far_rows = exchange(far_message, "pen", PEN, 3)
    swap_forward, own_forward = [near(pack([far], HINT["forward"]), 2) for far in (swap_far, own_far)]
    own_parts = call(
        functools.partial(own_rows_kernel, grid),
        [shape((2, fields, rows, lanes))] * 2,
        [],
        HINT["own"],
        [state, table],
            )
    own_fields, swap_fields = call(
        functools.partial(inverse_kernel, grid),
        [shape((grid, base_lanes))] * 2,
        [
            pltpu.VMEM((2, 4 * rows, lanes), f32),
            pltpu.VMEM((2, grid, base_lanes), bf16),
            pltpu.VMEM((2, grid, base_lanes), bf16),
            pltpu.VMEM(y_table.shape[1:], bf16),
            pltpu.SemaphoreType.DMA,
        ],
        HINT["inverse"],
        [near_rows, far_rows, came, *own_parts, table, jnp.asarray(y_table)],
        outside=(6,),
    )
    places = ((0, 0), (6, 0), (6, 1), (2, 0), (2, 1), (4, 0), (4, 1), (0, 1))
    packed = pack(
        [own_base, own_far, swap_far, own_near, swap_near, own_forward, swap_forward, came], HINT["pack"], (), EXTRA
    )
    partner = near(packed, 1)
    result = ()
    returns = []
    for field in range(2):
        messages = call(
            functools.partial(advection_kernel, places, field),
            [shape((2 * rows, 2 * lanes))] * PEN,
            [pltpu.VMEM((grid, 2 * lanes), bf16)] * 2,
            HINT["advect"][field],
            [own_fields, swap_fields, packed, partner, table],
        )
        returns.append(
            [messages[0]] + [exchange(messages[step], "pen", PEN, step) for step in range(1, PEN)]
        )
    for field, back in enumerate(returns):
        result = call(
            functools.partial(final_kernel, grid, field),
            [shape(state.shape)] * 2,
            [
                pltpu.VMEM((PEN, 2 * rows, 2 * lanes), f32),
                pltpu.VMEM((levels, rows, 2 * grid), f32),
                pltpu.VMEM((levels, rows, 2 * grid), f32),
                pltpu.SemaphoreType.DMA((2, levels)),
            ],
            HINT["final"] if field == 0 else 0,
            [*back, state, accum, table],
            into=result,
        )
    return tuple(result)


def solution(mesh):
    return jax.shard_map(
        functools.partial(on_device, dict(mesh.shape)),
        mesh=mesh,
        in_specs=(
            P(None, "ens", None, "pen", None),
            P(None, "ens", None, "pen", None),
            P(None, None, "pen", "ens"),
        ),
        out_specs=(P(None, "ens", None, "pen", None), P(None, "ens", None, "pen", None)),
        check_vma=False,
    )
```

profile of v0, /device:TPU:0, one launch (start us, length us, event | category | flops | bytes accessed | tf_op | source)
XLA Modules:
  0.0 42.8 jit_solution(4570269494377135494)
XLA Ops:
  0.6 0.0 copy-start.4
  0.6 1.0 %copy-done.4 = f32[6,4,64,32]{2,3,1,0:T(8,128)S(1)} copy-done((f32[6,4,64,32]{2,3,1,0:T(8,128)S(1)}, f32[6,4,64,32]{2,3,1,0:T(8,128)}, u32[]{:S(2)}) %copy-start.4) | copy-done | bytes 196632
  1.6 0.1 base_kernel.1
  1.7 6.0 %collective-permute-start.4 = (f32[32,768]{1,0:T(8,128)S(1)}, f32[32,768]{1,0:T(8,128)S(1)}, u32[]{:S(2)}, u32[]{:S(2)}) collective-permute-start(f32[32,768]{1,0:T(8,128)S(1)} %get-tuple-element.21.refs_0_), channel_id=1, source_target_pairs={{0,25},{1,24},{2,27},{3,26},{4,29},{5,28},{6,31},{7,30},{8,17},{9,... | collective-permute-start | bytes 294920 | tf_op jit(solution)/shard_map/ppermute | solution.py:512
  7.8 0.2 collective-permute-start.3
  8.0 0.0 copy-start.1
  8.0 1.2 %copy-done.1 = f32[2,1,4,64,512]{4,3,2,1,0:T(8,128)S(1)} copy-done((f32[2,1,4,64,512]{4,3,2,1,0:T(8,128)S(1)}, f32[2,1,4,64,512]{4,3,2,1,0:T(8,128)}, u32[]{:S(2)}) %copy-start.1) | copy-done | bytes 1048600
  9.3 1.6 %collective-permute-start = (f32[4,64,512]{2,1,0:T(8,128)S(1)}, f32[4,64,512]{2,1,0:T(8,128)S(1)}, u32[]{:S(2)}, u32[]{:S(2)}) collective-permute-start(f32[4,64,512]{2,1,0:T(8,128)S(1)} %get-tuple-element.23.refs_1_), channel_id=1, source_target_pairs={{0,2},{1,3},{2,0},{3,1},{4,6},{5,7},{6,4},{7,5},{8,10},{9,11},{10,... | collective-permute-start | bytes 1572872 | tf_op jit(solution)/shard_map/ppermute | solution.py:512
  10.9 0.1 collective-permute-start.5
  11.0 2.0 %collective-permute-start.6 = (f32[32,768]{1,0:T(8,128)S(1)}, f32[32,768]{1,0:T(8,128)S(1)}, u32[]{:S(2)}, u32[]{:S(2)}) collective-permute-start(f32[32,768]{1,0:T(8,128)S(1)} %pack_kernel.6), channel_id=1, source_target_pairs={{0,9},{1,8},{2,11},{3,10},{4,13},{5,12},{6,15},{7,14},{8,1},{9,0},... | collective-permute-start | bytes 294920 | tf_op jit(solution)/shard_map/ppermute | solution.py:512
  13.0 0.0 collective-permute-done.4.refs_0_.refs_2_
  13.0 1.5 %collective-permute-start.2 = (f32[40,768]{1,0:T(8,128)S(1)}, f32[40,768]{1,0:T(8,128)S(1)}, u32[]{:S(2)}, u32[]{:S(2)}) collective-permute-start(f32[40,768]{1,0:T(8,128)S(1)} %get-tuple-element.25), channel_id=1, source_target_pairs={{0,1},{1,0},{2,3},{3,2},{4,5},{5,4},{6,7},{7,6},{8,9},{9,8},{10,11... | collective-permute-start | bytes 368648 | tf_op jit(solution)/shard_map/ppermute | solution.py:512
  14.5 0.0 copy-start
  14.5 0.0 copy-start.2
  14.5 0.0 collective-permute-done.3.refs_0_.refs_1_
  14.5 2.4 %collective-permute-start.8 = (f32[32,768]{1,0:T(8,128)S(1)}, f32[32,768]{1,0:T(8,128)S(1)}, u32[]{:S(2)}, u32[]{:S(2)}) collective-permute-start(f32[32,768]{1,0:T(8,128)S(1)} %pack_kernel.8), channel_id=1, source_target_pairs={{0,8},{4,12},{8,0},{12,4},{16,24},{20,28},{24,16},{28,20},{1,9},{5... | collective-permute-start | bytes 294920 | tf_op jit(solution)/shard_map/ppermute | solution.py:512
  17.0 0.0 collective-permute-done.5.refs_3_
  17.0 0.6 %collective-permute-start.7 = (f32[32,768]{1,0:T(8,128)S(1)}, f32[32,768]{1,0:T(8,128)S(1)}, u32[]{:S(2)}, u32[]{:S(2)}) collective-permute-start(f32[32,768]{1,0:T(8,128)S(1)} %pack_kernel.7), channel_id=1, source_target_pairs={{0,8},{4,12},{8,0},{12,4},{16,24},{20,28},{24,16},{28,20},{1,9},{5... | collective-permute-start | bytes 294920 | tf_op jit(solution)/shard_map/ppermute | solution.py:512
  17.6 1.1 %collective-permute-done.6.refs_4_ = f32[32,768]{1,0:T(8,128)S(1)} collective-permute-done((f32[32,768]{1,0:T(8,128)S(1)}, f32[32,768]{1,0:T(8,128)S(1)}, u32[]{:S(2)}, u32[]{:S(2)}) %collective-permute-start.6) | collective-permute-done | bytes 98336 | tf_op jit(solution)/shard_map/ppermute | solution.py:512
  18.8 2.2 %collective-permute-start.1 = (f32[8,512]{1,0:T(8,128)S(1)}, f32[8,512]{1,0:T(8,128)S(1)}, u32[]{:S(2)}, u32[]{:S(2)}) collective-permute-start(f32[8,512]{1,0:T(8,128)S(1)} %get-tuple-element.24), channel_id=1, source_target_pairs={{0,3},{1,2},{2,1},{3,0},{4,7},{5,6},{6,5},{7,4},{8,11},{9,10},{10,... | collective-permute-start | bytes 49160 | tf_op jit(solution)/shard_map/ppermute | solution.py:512
  21.0 0.0 copy-done
  21.0 0.0 copy-done.2
  21.0 0.9 %own_rows_kernel.1 = (f32[2,6,64,128]{3,2,1,0:T(8,128)S(1)}, f32[2,6,64,128]{3,2,1,0:T(8,128)S(1)}) custom-call(f32[2,1,4,64,512]{4,3,2,1,0:T(8,128)S(1)} %copy-done.2, bf16[4,256,512]{2,1,0:T(8,128)(2,1)S(1)} %copy-done), custom_call_target="tpu_custom_call" | custom-call | bytes 2883584 | tf_op jit(solution)/shard_map/own_rows_kernel/pallas_call | solution.py:495
  21.8 0.0 copy-start.5
  21.8 0.0 collective-permute-done.2.refs_2_.refs_7_
  21.8 0.0 collective-permute-done.8.refs_6_
  21.9 0.5 %collective-permute-done.7.refs_5_ = f32[32,768]{1,0:T(8,128)S(1)} collective-permute-done((f32[32,768]{1,0:T(8,128)S(1)}, f32[32,768]{1,0:T(8,128)S(1)}, u32[]{:S(2)}, u32[]{:S(2)}) %collective-permute-start.7) | collective-permute-done | bytes 98336 | tf_op jit(solution)/shard_map/ppermute | solution.py:512
  22.4 0.1 pack_kernel.9.refs_2_
  22.4 0.1 collective-permute-start.9
  22.5 0.9 %collective-permute-done.1.refs_1_ = f32[8,512]{1,0:T(8,128)S(1)} collective-permute-done((f32[8,512]{1,0:T(8,128)S(1)}, f32[8,512]{1,0:T(8,128)S(1)}, u32[]{:S(2)}, u32[]{:S(2)}) %collective-permute-start.1) | collective-permute-done | bytes 16416 | tf_op jit(solution)/shard_map/ppermute | solution.py:512
  23.4 0.0 collective-permute-done.refs_0_
  23.4 0.0 copy-done.5
  23.4 2.3 %inverse_kernel.1 = (f32[256,768]{1,0:T(8,128)S(1)}, f32[256,768]{1,0:T(8,128)S(1)}) custom-call(f32[4,64,512]{2,1,0:T(8,128)S(1)} %collective-permute-done.refs_0_, f32[8,512]{1,0:T(8,128)S(1)} %collective-permute-done.1.refs_1_, f32[40,768]{1,0:T(8,128)S(1)} %collective-permute-done.2.refs_2_.refs_7_, f32[2,6,64,128]{3,2,1,0:T(8,128)S(1)} %get-tuple-element.26.refs_3_, ...), custom_call_target="tpu_custom_call" | custom-call | flops 10000000000 | bytes 5120000 | tf_op jit(solution)/shard_map/inverse_kernel/pallas_call | solution.py:495
  25.7 0.0 collective-permute-done.9.refs_3_
  25.7 0.5 %advection_kernel.3 = (f32[128,256]{1,0:T(8,128)S(1)}, f32[128,256]{1,0:T(8,128)S(1)}, f32[128,256]{1,0:T(8,128)S(1)}, f32[128,256]{1,0:T(8,128)S(1)}) custom-call(f32[256,768]{1,0:T(8,128)S(1)} %get-tuple-element.28.refs_0_, f32[256,768]{1,0:T(8,128)S(1)} %get-tuple-element.29.refs_1_, f32[256,768]{1,0:T(8,128)S(1)} %pack_kernel.9.refs_2_, ...), custom_call_target="tpu_custom_call" | custom-call | bytes 4718592 | tf_op jit(solution)/shard_map/advection_kernel/pallas_call | solution.py:495
  26.2 1.6 %collective-permute-start.13 = (f32[128,256]{1,0:T(8,128)S(1)}, f32[128,256]{1,0:T(8,128)S(1)}, u32[]{:S(2)}, u32[]{:S(2)}) collective-permute-start(f32[128,256]{1,0:T(8,128)S(1)} %get-tuple-element.35), channel_id=1, source_target_pairs={{0,1},{1,0},{2,3},{3,2},{4,5},{5,4},{6,7},{7,6},{8,9},{9,8},{10,11... | collective-permute-start | bytes 393224 | tf_op jit(solution)/shard_map/ppermute | solution.py:512
  27.8 1.3 %collective-permute-start.14 = (f32[128,256]{1,0:T(8,128)S(1)}, f32[128,256]{1,0:T(8,128)S(1)}, u32[]{:S(2)}, u32[]{:S(2)}) collective-permute-start(f32[128,256]{1,0:T(8,128)S(1)} %get-tuple-element.36), channel_id=1, source_target_pairs={{0,2},{1,3},{2,0},{3,1},{4,6},{5,7},{6,4},{7,5},{8,10},{9,11},{10,... | collective-permute-start | bytes 393224 | tf_op jit(solution)/shard_map/ppermute | solution.py:512
  29.1 0.0 copy-start.3
  29.1 0.7 %collective-permute-start.15 = (f32[128,256]{1,0:T(8,128)S(1)}, f32[128,256]{1,0:T(8,128)S(1)}, u32[]{:S(2)}, u32[]{:S(2)}) collective-permute-start(f32[128,256]{1,0:T(8,128)S(1)} %get-tuple-element.37), channel_id=1, source_target_pairs={{0,3},{1,2},{2,1},{3,0},{4,7},{5,6},{6,5},{7,4},{8,11},{9,10},{10,... | collective-permute-start | bytes 393224 | tf_op jit(solution)/shard_map/ppermute | solution.py:512
  29.8 0.5 %advection_kernel.2 = (f32[128,256]{1,0:T(8,128)S(1)}, f32[128,256]{1,0:T(8,128)S(1)}, f32[128,256]{1,0:T(8,128)S(1)}, f32[128,256]{1,0:T(8,128)S(1)}) custom-call(f32[256,768]{1,0:T(8,128)S(1)} %get-tuple-element.28.refs_0_, f32[256,768]{1,0:T(8,128)S(1)} %get-tuple-element.29.refs_1_, f32[256,768]{1,0:T(8,128)S(1)} %pack_kernel.9.refs_2_, ...), custom_call_target="tpu_custom_call" | custom-call | bytes 4718592 | tf_op jit(solution)/shard_map/advection_kernel/pallas_call | solution.py:495
  30.3 1.6 %collective-permute-start.10 = (f32[128,256]{1,0:T(8,128)S(1)}, f32[128,256]{1,0:T(8,128)S(1)}, u32[]{:S(2)}, u32[]{:S(2)}) collective-permute-start(f32[128,256]{1,0:T(8,128)S(1)} %get-tuple-element.31), channel_id=1, source_target_pairs={{0,1},{1,0},{2,3},{3,2},{4,5},{5,4},{6,7},{7,6},{8,9},{9,8},{10,11... | collective-permute-start | bytes 393224 | tf_op jit(solution)/shard_map/ppermute | solution.py:512
  31.8 1.3 %collective-permute-start.11 = (f32[128,256]{1,0:T(8,128)S(1)}, f32[128,256]{1,0:T(8,128)S(1)}, u32[]{:S(2)}, u32[]{:S(2)}) collective-permute-start(f32[128,256]{1,0:T(8,128)S(1)} %get-tuple-element.32), channel_id=1, source_target_pairs={{0,2},{1,3},{2,0},{3,1},{4,6},{5,7},{6,4},{7,5},{8,10},{9,11},{10,... | collective-permute-start | bytes 393224 | tf_op jit(solution)/shard_map/ppermute | solution.py:512
  33.1 0.0 collective-permute-done.13.refs_1_
  33.1 1.7 %collective-permute-start.12 = (f32[128,256]{1,0:T(8,128)S(1)}, f32[128,256]{1,0:T(8,128)S(1)}, u32[]{:S(2)}, u32[]{:S(2)}) collective-permute-start(f32[128,256]{1,0:T(8,128)S(1)} %get-tuple-element.33), channel_id=1, source_target_pairs={{0,3},{1,2},{2,1},{3,0},{4,7},{5,6},{6,5},{7,4},{8,11},{9,10},{10,... | collective-permute-start | bytes 393224 | tf_op jit(solution)/shard_map/ppermute | solution.py:512
  34.8 1.9 %collective-permute-done.14.refs_2_ = f32[128,256]{1,0:T(8,128)S(1)} collective-permute-done((f32[128,256]{1,0:T(8,128)S(1)}, f32[128,256]{1,0:T(8,128)S(1)}, u32[]{:S(2)}, u32[]{:S(2)}) %collective-permute-start.14) | collective-permute-done | bytes 131104 | tf_op jit(solution)/shard_map/ppermute | solution.py:512
  36.7 0.0 collective-permute-done.15.refs_3_
  36.7 0.0 copy-done.3
  36.7 1.9 %final_kernel.2 = (f32[2,1,4,64,512]{4,3,2,1,0:T(8,128)}, f32[2,1,4,64,512]{4,3,2,1,0:T(8,128)}) custom-call(f32[128,256]{1,0:T(8,128)S(1)} %get-tuple-element.34.refs_0_, f32[128,256]{1,0:T(8,128)S(1)} %collective-permute-done.13.refs_1_, f32[128,256]{1,0:T(8,128)S(1)} %collective-permute-done.14.refs_2_, f32[128,256]{1,0:T(8,128)S(1)} %collective-permute-done.15.refs_3_, ...), custom_call_target="tpu_custom_call" | custom-call | bytes 5767168 | tf_op jit(solution)/shard_map/final_kernel/pallas_call | solution.py:495
  38.6 0.0 collective-permute-done.10.refs_1_
  38.6 2.3 %collective-permute-done.11.refs_2_ = f32[128,256]{1,0:T(8,128)S(1)} collective-permute-done((f32[128,256]{1,0:T(8,128)S(1)}, f32[128,256]{1,0:T(8,128)S(1)}, u32[]{:S(2)}, u32[]{:S(2)}) %collective-permute-start.11) | collective-permute-done | bytes 131104 | tf_op jit(solution)/shard_map/ppermute | solution.py:512
  40.9 0.0 collective-permute-done.12.refs_3_
  40.9 1.9 %final_kernel.3 = (f32[2,1,4,64,512]{4,3,2,1,0:T(8,128)}, f32[2,1,4,64,512]{4,3,2,1,0:T(8,128)}) custom-call(f32[128,256]{1,0:T(8,128)S(1)} %get-tuple-element.30.refs_0_, f32[128,256]{1,0:T(8,128)S(1)} %collective-permute-done.10.refs_1_, f32[128,256]{1,0:T(8,128)S(1)} %collective-permute-done.11.refs_2_, ...), custom_call_target="tpu_custom_call", output_to_operand_aliasing={{0}: (7, {}), {1}: (8, {})} | custom-call | bytes 5767168 | tf_op jit(solution)/shard_map/final_kernel/pallas_call | solution.py:495
  (5 shorter events, 0.1 us)
Async XLA Ops:
  0.6 1.0 %copy-start.4 = (f32[6,4,64,32]{2,3,1,0:T(8,128)S(1)}, f32[6,4,64,32]{2,3,1,0:T(8,128)}, u32[]{:S(2)}) copy-start(f32[6,4,64,32]{2,3,1,0:T(8,128)} %param.7) | copy-start | bytes 589828
  1.7 11.3 %collective-permute-start.4 = (f32[32,768]{1,0:T(8,128)S(1)}, f32[32,768]{1,0:T(8,128)S(1)}, u32[]{:S(2)}, u32[]{:S(2)}) collective-permute-start(f32[32,768]{1,0:T(8,128)S(1)} %get-tuple-element.21.refs_0_), channel_id=1, source_target_pairs={{0,25},{1,24},{2,27},{3,26},{4,29},{5,28},{6,31},{7,30},{8,17},{9,... | collective-permute-start | bytes 294920 | tf_op jit(solution)/shard_map/ppermute | solution.py:512
  7.8 6.7 %collective-permute-start.3 = (f32[32,768]{1,0:T(8,128)S(1)}, f32[32,768]{1,0:T(8,128)S(1)}, u32[]{:S(2)}, u32[]{:S(2)}) collective-permute-start(f32[32,768]{1,0:T(8,128)S(1)} %get-tuple-element.22.refs_2_.refs_0_), channel_id=1, source_target_pairs={{0,24},{4,28},{8,16},{12,20},{16,8},{20,12},{24,0},{28,4},{1,25},{... | collective-permute-start | bytes 294920 | tf_op jit(solution)/shard_map/ppermute | solution.py:512
  8.0 1.2 %copy-start.1 = (f32[2,1,4,64,512]{4,3,2,1,0:T(8,128)S(1)}, f32[2,1,4,64,512]{4,3,2,1,0:T(8,128)}, u32[]{:S(2)}) copy-start(f32[2,1,4,64,512]{4,3,2,1,0:T(8,128)} %refs_4_.5) | copy-start | bytes 3145732
  9.3 14.1 %collective-permute-start = (f32[4,64,512]{2,1,0:T(8,128)S(1)}, f32[4,64,512]{2,1,0:T(8,128)S(1)}, u32[]{:S(2)}, u32[]{:S(2)}) collective-permute-start(f32[4,64,512]{2,1,0:T(8,128)S(1)} %get-tuple-element.23.refs_1_), channel_id=1, source_target_pairs={{0,2},{1,3},{2,0},{3,1},{4,6},{5,7},{6,4},{7,5},{8,10},{9,11},{10,... | collective-permute-start | bytes 1572872 | tf_op jit(solution)/shard_map/ppermute | solution.py:512
  10.9 6.1 %collective-permute-start.5 = (f32[32,768]{1,0:T(8,128)S(1)}, f32[32,768]{1,0:T(8,128)S(1)}, u32[]{:S(2)}, u32[]{:S(2)}) collective-permute-start(f32[32,768]{1,0:T(8,128)S(1)} %pack_kernel.5), channel_id=1, source_target_pairs={{0,8},{4,12},{8,0},{12,4},{16,24},{20,28},{24,16},{28,20},{1,9},{5... | collective-permute-start | bytes 294920 | tf_op jit(solution)/shard_map/ppermute | solution.py:512
  11.0 7.8 %collective-permute-start.6 = (f32[32,768]{1,0:T(8,128)S(1)}, f32[32,768]{1,0:T(8,128)S(1)}, u32[]{:S(2)}, u32[]{:S(2)}) collective-permute-start(f32[32,768]{1,0:T(8,128)S(1)} %pack_kernel.6), channel_id=1, source_target_pairs={{0,9},{1,8},{2,11},{3,10},{4,13},{5,12},{6,15},{7,14},{8,1},{9,0},... | collective-permute-start | bytes 294920 | tf_op jit(solution)/shard_map/ppermute | solution.py:512
  13.0 8.8 %collective-permute-start.2 = (f32[40,768]{1,0:T(8,128)S(1)}, f32[40,768]{1,0:T(8,128)S(1)}, u32[]{:S(2)}, u32[]{:S(2)}) collective-permute-start(f32[40,768]{1,0:T(8,128)S(1)} %get-tuple-element.25), channel_id=1, source_target_pairs={{0,1},{1,0},{2,3},{3,2},{4,5},{5,4},{6,7},{7,6},{8,9},{9,8},{10,11... | collective-permute-start | bytes 368648 | tf_op jit(solution)/shard_map/ppermute | solution.py:512
  14.5 6.4 %copy-start = (bf16[4,256,512]{2,1,0:T(8,128)(2,1)S(1)}, bf16[4,256,512]{2,1,0:T(8,128)(2,1)}, u32[]{:S(2)}) copy-start(bf16[4,256,512]{2,1,0:T(8,128)(2,1)} %constant.4.clone.refs_1_.refs_5_.refs_4_.refs_6_) | copy-start | bytes 3145732
  14.5 6.4 %copy-start.2 = (f32[2,1,4,64,512]{4,3,2,1,0:T(8,128)S(1)}, f32[2,1,4,64,512]{4,3,2,1,0:T(8,128)}, u32[]{:S(2)}) copy-start(f32[2,1,4,64,512]{4,3,2,1,0:T(8,128)} %refs_4_.5) | copy-start | bytes 3145732
  14.5 7.3 %collective-permute-start.8 = (f32[32,768]{1,0:T(8,128)S(1)}, f32[32,768]{1,0:T(8,128)S(1)}, u32[]{:S(2)}, u32[]{:S(2)}) collective-permute-start(f32[32,768]{1,0:T(8,128)S(1)} %pack_kernel.8), channel_id=1, source_target_pairs={{0,8},{4,12},{8,0},{12,4},{16,24},{20,28},{24,16},{28,20},{1,9},{5... | collective-permute-start | bytes 294920 | tf_op jit(solution)/shard_map/ppermute | solution.py:512
  17.0 5.4 %collective-permute-start.7 = (f32[32,768]{1,0:T(8,128)S(1)}, f32[32,768]{1,0:T(8,128)S(1)}, u32[]{:S(2)}, u32[]{:S(2)}) collective-permute-start(f32[32,768]{1,0:T(8,128)S(1)} %pack_kernel.7), channel_id=1, source_target_pairs={{0,8},{4,12},{8,0},{12,4},{16,24},{20,28},{24,16},{28,20},{1,9},{5... | collective-permute-start | bytes 294920 | tf_op jit(solution)/shard_map/ppermute | solution.py:512
  18.8 4.6 %collective-permute-start.1 = (f32[8,512]{1,0:T(8,128)S(1)}, f32[8,512]{1,0:T(8,128)S(1)}, u32[]{:S(2)}, u32[]{:S(2)}) collective-permute-start(f32[8,512]{1,0:T(8,128)S(1)} %get-tuple-element.24), channel_id=1, source_target_pairs={{0,3},{1,2},{2,1},{3,0},{4,7},{5,6},{6,5},{7,4},{8,11},{9,10},{10,... | collective-permute-start | bytes 49160 | tf_op jit(solution)/shard_map/ppermute | solution.py:512
  21.8 1.6 %copy-start.5 = (bf16[4,2,256,256]{3,2,1,0:T(8,128)(2,1)S(1)}, bf16[4,2,256,256]{3,2,1,0:T(8,128)(2,1)}, u32[]{:S(2)}) copy-start(bf16[4,2,256,256]{3,2,1,0:T(8,128)(2,1)} %constant.5.clone.refs_6_) | copy-start | bytes 3145732
  22.4 3.3 %collective-permute-start.9 = (f32[256,768]{1,0:T(8,128)S(1)}, f32[256,768]{1,0:T(8,128)S(1)}, u32[]{:S(2)}, u32[]{:S(2)}) collective-permute-start(f32[256,768]{1,0:T(8,128)S(1)} %pack_kernel.9.refs_2_), channel_id=1, source_target_pairs={{0,4},{4,0},{8,12},{12,8},{16,20},{20,16},{24,28},{28,24},{1,5},{5... | collective-permute-start | bytes 2359304 | tf_op jit(solution)/shard_map/ppermute | solution.py:512
  26.2 6.9 %collective-permute-start.13 = (f32[128,256]{1,0:T(8,128)S(1)}, f32[128,256]{1,0:T(8,128)S(1)}, u32[]{:S(2)}, u32[]{:S(2)}) collective-permute-start(f32[128,256]{1,0:T(8,128)S(1)} %get-tuple-element.35), channel_id=1, source_target_pairs={{0,1},{1,0},{2,3},{3,2},{4,5},{5,4},{6,7},{7,6},{8,9},{9,8},{10,11... | collective-permute-start | bytes 393224 | tf_op jit(solution)/shard_map/ppermute | solution.py:512
  27.8 8.9 %collective-permute-start.14 = (f32[128,256]{1,0:T(8,128)S(1)}, f32[128,256]{1,0:T(8,128)S(1)}, u32[]{:S(2)}, u32[]{:S(2)}) collective-permute-start(f32[128,256]{1,0:T(8,128)S(1)} %get-tuple-element.36), channel_id=1, source_target_pairs={{0,2},{1,3},{2,0},{3,1},{4,6},{5,7},{6,4},{7,5},{8,10},{9,11},{10,... | collective-permute-start | bytes 393224 | tf_op jit(solution)/shard_map/ppermute | solution.py:512
  29.1 7.7 %copy-start.3 = (f32[2,1,4,64,512]{4,3,2,1,0:T(8,128)S(1)}, f32[2,1,4,64,512]{4,3,2,1,0:T(8,128)}, u32[]{:S(2)}) copy-start(f32[2,1,4,64,512]{4,3,2,1,0:T(8,128)} %refs_5_.4) | copy-start | bytes 3145732
  29.1 7.7 %collective-permute-start.15 = (f32[128,256]{1,0:T(8,128)S(1)}, f32[128,256]{1,0:T(8,128)S(1)}, u32[]{:S(2)}, u32[]{:S(2)}) collective-permute-start(f32[128,256]{1,0:T(8,128)S(1)} %get-tuple-element.37), channel_id=1, source_target_pairs={{0,3},{1,2},{2,1},{3,0},{4,7},{5,6},{6,5},{7,4},{8,11},{9,10},{10,... | collective-permute-start | bytes 393224 | tf_op jit(solution)/shard_map/ppermute | solution.py:512
  30.3 8.3 %collective-permute-start.10 = (f32[128,256]{1,0:T(8,128)S(1)}, f32[128,256]{1,0:T(8,128)S(1)}, u32[]{:S(2)}, u32[]{:S(2)}) collective-permute-start(f32[128,256]{1,0:T(8,128)S(1)} %get-tuple-element.31), channel_id=1, source_target_pairs={{0,1},{1,0},{2,3},{3,2},{4,5},{5,4},{6,7},{7,6},{8,9},{9,8},{10,11... | collective-permute-start | bytes 393224 | tf_op jit(solution)/shard_map/ppermute | solution.py:512
  31.8 9.1 %collective-permute-start.11 = (f32[128,256]{1,0:T(8,128)S(1)}, f32[128,256]{1,0:T(8,128)S(1)}, u32[]{:S(2)}, u32[]{:S(2)}) collective-permute-start(f32[128,256]{1,0:T(8,128)S(1)} %get-tuple-element.32), channel_id=1, source_target_pairs={{0,2},{1,3},{2,0},{3,1},{4,6},{5,7},{6,4},{7,5},{8,10},{9,11},{10,... | collective-permute-start | bytes 393224 | tf_op jit(solution)/shard_map/ppermute | solution.py:512
  33.1 7.8 %collective-permute-start.12 = (f32[128,256]{1,0:T(8,128)S(1)}, f32[128,256]{1,0:T(8,128)S(1)}, u32[]{:S(2)}, u32[]{:S(2)}) collective-permute-start(f32[128,256]{1,0:T(8,128)S(1)} %get-tuple-element.33), channel_id=1, source_target_pairs={{0,3},{1,2},{2,1},{3,0},{4,7},{5,6},{6,5},{7,4},{8,11},{9,10},{10,... | collective-permute-start | bytes 393224 | tf_op jit(solution)/shard_map/ppermute | solution.py:512
where the time goes:
time: 43 us; the launch traced here: 42.8 us
  starting transfers between devices  24.9 us (58%)
  Pallas kernels  8.09 us (19%)
  waiting for transfers between devices  6.8 us (16%)
  local copies, waits for them, and re-layouts  2.23 us (5%)
  between operations  0.79 us (2%)
    ppermute x16, starting transfers between devices, exchange(): lax.ppermute(values, axis, [(index, index ^ mask) for index in range(size)])  24.9 us
    pallas_call x13, Pallas kernels, call(): pl.pallas_call(lambda *refs: kernel(*refs[:count], *refs[total:]), out_sh...  8.09 us
    ppermute x16, waiting for transfers between devices, exchange(): lax.ppermute(values, axis, [(index, index ^ mask) for index in range(size)])  6.8 us
    unnamed x12, local copies, waits for them, and re-layouts  2.23 us
  transfers between devices with their start and end apart: 16, of which 5 were waited for; matrix products, arithmetic and copies ran while one was open for 0% of the time, Pallas kernels for 13%

commit v1 on v0

--- a/solution.py
+++ b/solution.py
@@ -177,7 +177,8 @@
 
 PEN = 4
 EXTRA = 8
-HINT = dict(own=0, inverse=10**10, forward=10**10, pack=0, advect=(0, 0), final=0)
+NEAR_X = 16
+HINT = dict(own=0, inverse=10**10, forward=5 * 10**9, early=0, pack=0, advect=(0, 0), linear=0)
 
 
 def split(values):
@@ -203,6 +204,12 @@
     kx = np.arange(grid)
     x = kx[:, None]
     return split_table(np.concatenate([cosine(grid, x, kx), sine(grid, x, kx)], axis=1))
+
+
+def row_numbers(device, rows):
+    own = device * rows + np.arange(rows)
+    near = [(device ^ step) * rows + np.arange(count) for step, count in ((1, NEAR_X), (2, rows - NEAR_X))]
+    return np.concatenate([own] + near)
 
 
 def y_inverse_table(grid):
@@ -210,15 +217,18 @@
     y = np.arange(grid)[:, None]
     tables = []
     for device in range(PEN):
-        ky = np.concatenate([block * rows + np.arange(rows) for block in (device, device ^ 2)])
+        ky = row_numbers(device, rows)
         real = np.where(ky % (grid // 2) == 0, 1.0, 2.0) * cosine(grid, y, ky)
         imag = -2.0 * sine(grid, y, ky)
-        near, far = (device ^ 1) * rows, (device ^ 3) * rows
+        extra = (device ^ 1) * rows + NEAR_X
+        far = (device ^ 3) * rows
+        from_y = rows + NEAR_X
+        extra_real, extra_imag = 2.0 * cosine(grid, y[:, 0], extra), -2.0 * sine(grid, y[:, 0], extra)
+        imag[:, from_y] = extra_imag
         if device % 2 == 0:
-            imag[:, 0] = 2.0 * cosine(grid, y[:, 0], near)
-            imag[:, rows] = -2.0 * sine(grid, y[:, 0], near)
+            imag[:, 0] = extra_real
         else:
-            real[:, rows] = cosine(grid, y[:, 0], near)
+            real[:, from_y] = extra_real
             imag[:, rows] = cosine(grid, y[:, 0], far)
         tables.append(np.concatenate([real, imag], axis=1))
     return split_table(np.stack(tables))
@@ -277,16 +287,23 @@
 
 def near_kernel(block_ref, state_ref, swap_ref, near_ref, far_ref):
     mine = (lax.axis_index("pen") % 2) * 2
-    tall = block_ref.shape[0]
-    swap_ref[:tall, :] = block_ref[...]
-    swap_ref[tall:, :] = jnp.zeros((EXTRA, swap_ref.shape[1]), jnp.float32)
+    width = swap_ref.shape[1]
+    tall, lanes = block_ref.shape
+    swap_ref[:tall, :] = block_ref[:, :width]
+    half = tall // 2
+    swap_ref[tall : tall + half, : lanes - width] = block_ref[:half, width:]
+    swap_ref[tall : tall + half, lanes - width :] = block_ref[half:, width:]
+    start = tall + half
+    swap_ref[start + 4 * NEAR_X :, :] = jnp.zeros((EXTRA, width), jnp.float32)
     far_ref[...] = jnp.zeros_like(far_ref)
     for index in range(4):
         field, level = index // 2, index % 2
-        line = state_ref[field, 0, 2 - mine + level, 0:1, :]
-        near_ref[index] = state_ref[field, 0, mine + level]
-        far_ref[index : index + 1, :] = line
-        swap_ref[tall + index : tall + index + 1, : far_ref.shape[1]] = line
+        rows = state_ref[field, 0, 2 - mine + level, : NEAR_X + EXTRA, :]
+        swap_ref[start + NEAR_X * index : start + NEAR_X * (index + 1), :] = rows[:NEAR_X]
+        line = start + 4 * NEAR_X + index
+        swap_ref[line : line + 1, :] = rows[NEAR_X : NEAR_X + 1]
+        far_ref[index : index + 1, :] = rows[:1]
+        near_ref[index] = state_ref[field, 0, mine + level, : near_ref.shape[1], :]
 
 
 def x_stage(grid, table, ky, held):
@@ -348,12 +365,13 @@
     pen = lax.axis_index("pen")
     odd = pen % 2 == 1
     count = rows + EXTRA
-    tall = came_ref.shape[0] - EXTRA
+    start = came_ref.shape[0] - 4 * NEAR_X - EXTRA
     held = [
         jnp.concatenate(
             [
+                came_ref[start + NEAR_X * index : start + NEAR_X * (index + 1), :],
                 near_ref[index],
-                came_ref[tall + index : tall + index + 1, : 2 * grid],
+                came_ref[start + 4 * NEAR_X + index : start + 4 * NEAR_X + index + 1, :],
                 far_ref[index : index + 1, :],
                 jnp.zeros((EXTRA - 2, 2 * grid), jnp.float32),
             ],
@@ -362,8 +380,10 @@
         for index in range(4)
     ]
     row = lax.broadcasted_iota(jnp.int32, (count, 1), 0)
-    ky = jnp.where(row < rows, (pen ^ 2) * rows + row, (pen ^ 1) * rows)
+    ky = jnp.where(row < NEAR_X, (pen ^ 1) * rows + row, (pen ^ 2) * rows + row - NEAR_X)
+    ky = jnp.where(row == rows, (pen ^ 1) * rows + NEAR_X, ky)
     ky = jnp.where(row > rows, (pen ^ 3) * rows, ky)
+    from_y = rows + NEAR_X
     for number, results in enumerate(x_stage(grid, x_columns(grid, x_ref), ky, held)):
         for level, (real, imag) in enumerate(results):
             first_imag = own_imag[level, number, 0:1, :]
@@ -371,11 +391,14 @@
             mixed[level, rows : 2 * rows, :] = real[:rows]
             mixed[level, 2 * rows : 3 * rows, :] = own_imag[level, number]
             mixed[level, 3 * rows :, :] = imag[:rows]
-            near_real, near_imag = real[rows : rows + 1], imag[rows : rows + 1]
+            extra_real, extra_imag = real[rows : rows + 1], imag[rows : rows + 1]
             far_real = real[rows + 1 : rows + 2]
-            mixed[level, rows : rows + 1, :] = jnp.where(odd, near_real, real[0:1])
-            mixed[level, 2 * rows : 2 * rows + 1, :] = jnp.where(odd, first_imag, near_real)
-            mixed[level, 3 * rows : 3 * rows + 1, :] = jnp.where(odd, far_real, near_imag)
+            mixed[level, from_y : from_y + 1, :] = jnp.where(
+                odd, extra_real, real[NEAR_X : NEAR_X + 1]
+            )
+            mixed[level, 2 * rows : 2 * rows + 1, :] = jnp.where(odd, first_imag, extra_real)
+            mixed[level, 3 * rows : 3 * rows + 1, :] = jnp.where(odd, far_real, imag[0:1])
+            mixed[level, 2 * rows + from_y : 2 * rows + from_y + 1, :] = extra_imag
         for block, values in enumerate(interleave(mixed[0], mixed[1])):
             high, low = split(values)
             high_ref[block ^ (pen % 2), :, 128 * number : 128 * number + 128] = high
@@ -387,16 +410,17 @@
 
 
 def advection_kernel(places, field, own_ref, swap_ref, *refs):
-    packs, (table_ref, *outs, high_ref, low_ref) = refs[:2], refs[2:]
+    packs, (table_ref, *outs, high_ref, low_ref) = refs[:4], refs[4:]
     ens = lax.axis_index("ens")
-    tall = packs[0].shape[0] // len(places)
-    for which in range(2):
-        for slot, (offset, chunk) in enumerate(places):
+    for group, which in [(group, which) for group in range(2) for which in range(2)]:
+        pack_ref = packs[2 * group + which]
+        tall = pack_ref.shape[0] // len(places[group])
+        for slot, (offset, chunk) in enumerate(places[group]):
             place = pl.ds(pl.multiple_of((ens ^ offset ^ which) * tall, tall), tall)
             along_ref = (own_ref, swap_ref)[chunk]
 
-            def base(index, which=which, slot=slot):
-                return packs[which][tall * slot : tall * (slot + 1), 128 * index : 128 * index + 128]
+            def base(index, pack_ref=pack_ref, slot=slot, tall=tall):
+                return pack_ref[tall * slot : tall * (slot + 1), 128 * index : 128 * index + 128]
 
             def along(index, place=place, along_ref=along_ref):
                 return along_ref[place, 128 * index : 128 * index + 128]
@@ -422,15 +446,34 @@
         )
 
 
+def linear_kernel(grid, state_ref, accum_ref, out_ref):
+    rows, levels = state_ref.shape[3], state_ref.shape[2]
+    row = lax.broadcasted_iota(jnp.int32, (rows, 1), 0)
+    _, kappa_x, square, inverse = wave_arrays(lax.axis_index("pen") * rows + row, grid)
+    real, imag = slice(0, grid), slice(grid, 2 * grid)
+    for field in range(2):
+        factor = kappa_x * buoyancy_gain if field == 0 else kappa_x * inverse * stratification
+        damping = (viscosity if field == 0 else diffusivity) * square
+        for level in range(levels):
+            for columns, other, sign in ((real, imag, 1.0), (imag, real, -1.0)):
+                here = state_ref[field, 0, level, :, columns]
+                above = state_ref[field, 0, min(level + 1, levels - 1), :, columns]
+                below = state_ref[field, 0, max(level - 1, 0), :, columns]
+                out_ref[field, 0, level, :, columns] = (
+                    memory_factor * accum_ref[field, 0, level, :, columns]
+                    - sign * factor * state_ref[1 - field, 0, level, :, other]
+                    - damping * here
+                    + vertical_mixing * (above + below - 2.0 * here)
+                )
+
+
 def final_kernel(grid, field, *refs):
-    messages, (state_ref, accum_ref, table_ref) = refs[:PEN], refs[PEN : PEN + 3]
+    messages, (state_ref, part_ref, table_ref) = refs[:PEN], refs[PEN : PEN + 3]
     state_out, accum_out, gathered, state_next, accum_next, sems = refs[-6:]
     rows, levels = state_ref.shape[3], state_ref.shape[2]
     pen = lax.axis_index("pen")
     for step in range(PEN):
         gathered[pen ^ step] = messages[step][...]
-    row = lax.broadcasted_iota(jnp.int32, (rows, 1), 0)
-    _, kappa_x, square, inverse = wave_arrays(pen * rows + row, grid)
     table = (table_ref[0], table_ref[1])
     real, imag = slice(0, grid), slice(grid, 2 * grid)
     copies = []
@@ -447,28 +490,15 @@
         for level in (2 * pair, 2 * pair + 1):
             start = 2 * rows * (level - 2 * pair)
             top, bottom = product[start : start + rows], product[start + rows : start + 2 * rows]
-            for columns, other, sign, advect in (
-                (real, imag, 1.0, top[:, :grid] + bottom[:, grid:]),
-                (imag, real, -1.0, bottom[:, :grid] - top[:, grid:]),
+            for columns, advect in (
+                (real, top[:, :grid] + bottom[:, grid:]),
+                (imag, bottom[:, :grid] - top[:, grid:]),
             ):
-                here = state_ref[field, 0, level, :, columns]
-                above = state_ref[field, 0, min(level + 1, levels - 1), :, columns]
-                below = state_ref[field, 0, max(level - 1, 0), :, columns]
-                cross = state_ref[1 - field, 0, level, :, other]
-                if field == 0:
-                    coupling = (-sign * buoyancy_gain) * (kappa_x * cross)
-                else:
-                    coupling = (-sign * stratification) * (kappa_x * inverse * cross)
-                damping = viscosity if field == 0 else diffusivity
-                memory = (
-                    memory_factor * accum_ref[field, 0, level, :, columns]
-                    - advect
-                    + coupling
-                    - damping * square * here
-                    + vertical_mixing * (above + below - 2.0 * here)
+                memory = part_ref[field, 0, level, :, columns] - advect
+                accum_next[level, :, columns] = memory
+                state_next[level, :, columns] = (
+                    state_ref[field, 0, level, :, columns] + weight_factor * time_step * memory
                 )
-                accum_next[level, :, columns] = memory
-                state_next[level, :, columns] = here + weight_factor * time_step * memory
             for which, (held, out) in enumerate(((state_next, state_out), (accum_next, accum_out))):
                 copy = pltpu.make_async_copy(
                     held.at[level], out.at[field, 0, level], sems.at[which, level]
@@ -480,11 +510,19 @@
 
 
 def pack_kernel(*refs):
-    start, total = 0, refs[-1].shape[0]
+    start, packed = 0, refs[-1]
+    lanes = packed.shape[1]
     for ref in refs[:-1]:
-        count = min(ref.shape[0], total - start)
-        refs[-1][start : start + count, :] = ref[:count, :]
-        start += count
+        count, width = ref.shape
+        if width == lanes:
+            packed[start : start + count, :] = ref[...]
+            start += count
+        else:
+            tall = packed.shape[0] - start
+            half = tall // 2
+            packed[start:, :width] = ref[:tall, :]
+            packed[start : start + half, width:] = ref[tall : tall + half, : lanes - width]
+            packed[start + half :, width:] = ref[tall : tall + half, lanes - width :]
 
 
 def call(kernel, outs, scratch, cost, args, after=(), into=None, outside=()):
@@ -512,9 +550,9 @@
     return lax.ppermute(values, axis, [(index, index ^ mask) for index in range(size)])
 
 
-def pack(arrays, cost=0, after=(), drop=0):
-    total = sum(array.shape[0] for array in arrays) - drop
-    shape = jax.ShapeDtypeStruct((total, arrays[0].shape[1]), arrays[0].dtype)
+def pack(arrays, cost=0, after=(), rows=None):
+    rows = rows or sum(array.shape[0] for array in arrays)
+    shape = jax.ShapeDtypeStruct((rows, arrays[0].shape[1]), arrays[0].dtype)
     return call(pack_kernel, [shape], [], cost, arrays, after=after)[0]
 
 
@@ -541,26 +579,28 @@
         base_kernel, [shape((tall, base_lanes))] * 2, [], 0, [jnp.swapaxes(base_flow, 2, 3)]
     )
     own_far, swap_far = near(own_base, 6), across(swap_base, 6)
+    message = tall + tall // 2 + 4 * NEAR_X + EXTRA
     swap_message, rows_message, far_message = call(
         near_kernel,
-        [shape((tall + EXTRA, base_lanes)), shape((4, rows, 2 * grid)), shape((EXTRA, 2 * grid))],
+        [shape((message, 2 * grid)), shape((4, rows - NEAR_X, 2 * grid)), shape((EXTRA, 2 * grid))],
         [],
         0,
         [swap_base, state],
         after=[own_base],
     )
     near_rows = exchange(rows_message, "pen", PEN, 2)
-    own_near = near(pack([own_base], after=[rows_message]), 2)
     swap_near = across(pack([swap_base], after=[rows_message]), 2)
     came = exchange(swap_message, "pen", PEN, 1)
     far_rows = exchange(far_message, "pen", PEN, 3)
-    swap_forward, own_forward = [near(pack([far], HINT["forward"]), 2) for far in (swap_far, own_far)]
+    swap_forward = near(pack([swap_far], HINT["forward"]), 2)
+    own_forward = near(pack([own_far, own_base], HINT["forward"]), 2)
     own_parts = call(
         functools.partial(own_rows_kernel, grid),
         [shape((2, fields, rows, lanes))] * 2,
         [],
         HINT["own"],
         [state, table],
+        after=[swap_far],
             )
     own_fields, swap_fields = call(
         functools.partial(inverse_kernel, grid),
@@ -576,24 +616,40 @@
         [near_rows, far_rows, came, *own_parts, table, jnp.asarray(y_table)],
         outside=(6,),
     )
-    places = ((0, 0), (6, 0), (6, 1), (2, 0), (2, 1), (4, 0), (4, 1), (0, 1))
-    packed = pack(
-        [own_base, own_far, swap_far, own_near, swap_near, own_forward, swap_forward, came], HINT["pack"], (), EXTRA
-    )
-    partner = near(packed, 1)
-    result = ()
-    returns = []
+    places = (((0, 0), (6, 0), (6, 1), (2, 1)), ((4, 0), (2, 0), (4, 1), (0, 1)))
+    packs = []
+    for (blocks, cost, after), group in zip(
+        (
+            ([own_base, own_far, swap_far, swap_near], HINT["early"], ()),
+            ([own_forward, swap_forward, came], HINT["pack"], ()),
+        ),
+        places,
+        strict=True,
+    ):
+        packed = pack(blocks, cost, after, len(group) * tall)
+        packs += [packed, near(packed, 1)]
+    returns, made = [], []
     for field in range(2):
         messages = call(
             functools.partial(advection_kernel, places, field),
             [shape((2 * rows, 2 * lanes))] * PEN,
             [pltpu.VMEM((grid, 2 * lanes), bf16)] * 2,
             HINT["advect"][field],
-            [own_fields, swap_fields, packed, partner, table],
+            [own_fields, swap_fields, *packs, table],
         )
+        made.append(messages[0])
         returns.append(
             [messages[0]] + [exchange(messages[step], "pen", PEN, step) for step in range(1, PEN)]
         )
+    (part,) = call(
+        functools.partial(linear_kernel, grid),
+        [shape(state.shape)],
+        [],
+        HINT["linear"],
+        [state, accum],
+        after=made[1:],
+    )
+    result = ()
     for field, back in enumerate(returns):
         result = call(
             functools.partial(final_kernel, grid, field),
@@ -604,8 +660,8 @@
                 pltpu.VMEM((levels, rows, 2 * grid), f32),
                 pltpu.SemaphoreType.DMA((2, levels)),
             ],
-            HINT["final"] if field == 0 else 0,
-            [*back, state, accum, table],
+            0,
+            [*back, state, part, table],
             into=result,
         )
     return tuple(result)

time: 43 us -> 42.5 us (0.988)
  starting transfers between devices: 24.9 us -> 23.1 us
  waiting for transfers between devices: 6.8 us -> 8.02 us
    ppermute x16, starting transfers between devices: 24.9 us -> 23.1 us  [exchange(): lax.ppermute(values, axis, [(index, index ^ mask) for index in range(size)])]
    ppermute x16, waiting for transfers between devices: 6.8 us -> 8.02 us  [exchange(): lax.ppermute(values, axis, [(index, index ^ mask) for index in range(size)])]
    pallas_call x13 -> x14, Pallas kernels: 8.09 us -> 8.19 us  [call(): pl.pallas_call(lambda *refs: kernel(*refs[:count], *refs[total:]), out_sh...]
  transfers between devices with their start and end apart: 16 -> 16, of which waited for: 5 -> 6; matrix products, arithmetic and copies ran while one was open for 0% -> 0% of each run, Pallas kernels for 13% -> 14%
where the time goes in v1:
time: 42.5 us; the launch traced here: 42.3 us
  starting transfers between devices  23.1 us (54%)
  Pallas kernels  8.19 us (19%)
  waiting for transfers between devices  8.02 us (19%)
  local copies, waits for them, and re-layouts  2.23 us (5%)
  between operations  0.78 us (2%)
    ppermute x16, starting transfers between devices, exchange(): lax.ppermute(values, axis, [(index, index ^ mask) for index in range(size)])  23.1 us
    pallas_call x14, Pallas kernels, call(): pl.pallas_call(lambda *refs: kernel(*refs[:count], *refs[total:]), out_sh...  8.19 us
    ppermute x16, waiting for transfers between devices, exchange(): lax.ppermute(values, axis, [(index, index ^ mask) for index in range(size)])  8.02 us
    unnamed x12, local copies, waits for them, and re-layouts  2.23 us
  transfers between devices with their start and end apart: 16, of which 6 were waited for; matrix products, arithmetic and copies ran while one was open for 0% of the time, Pallas kernels for 14%

profile of v1, /device:TPU:0, one launch (start us, length us, event | category | flops | bytes accessed | tf_op | source)
XLA Modules:
  0.0 42.3 jit_solution(8768876224513607438)
XLA Ops:
  0.6 0.0 copy-start.4
  0.6 1.0 %copy-done.4 = f32[6,4,64,32]{2,3,1,0:T(8,128)S(1)} copy-done((f32[6,4,64,32]{2,3,1,0:T(8,128)S(1)}, f32[6,4,64,32]{2,3,1,0:T(8,128)}, u32[]{:S(2)}) %copy-start.4) | copy-done | bytes 196632
  1.6 0.1 base_kernel.1
  1.7 5.1 %collective-permute-start.4 = (f32[32,768]{1,0:T(8,128)S(1)}, f32[32,768]{1,0:T(8,128)S(1)}, u32[]{:S(2)}, u32[]{:S(2)}) collective-permute-start(f32[32,768]{1,0:T(8,128)S(1)} %get-tuple-element.22.refs_2_.refs_0_.refs_1_), channel_id=1, source_target_pairs={{0,24},{4,28},{8,16},{12,20},{16,8},{20,12},{24,0},{28,4},{1,25},{... | collective-permute-start | bytes 294920 | tf_op jit(solution)/shard_map/ppermute | solution.py:550
  6.9 1.1 %collective-permute-start.3 = (f32[32,768]{1,0:T(8,128)S(1)}, f32[32,768]{1,0:T(8,128)S(1)}, u32[]{:S(2)}, u32[]{:S(2)}) collective-permute-start(f32[32,768]{1,0:T(8,128)S(1)} %get-tuple-element.21.refs_0_), channel_id=1, source_target_pairs={{0,25},{1,24},{2,27},{3,26},{4,29},{5,28},{6,31},{7,30},{8,17},{9,... | collective-permute-start | bytes 294920 | tf_op jit(solution)/shard_map/ppermute | solution.py:550
  8.0 0.0 copy-start
  8.0 1.2 %copy-done = f32[2,1,4,64,512]{4,3,2,1,0:T(8,128)S(1)} copy-done((f32[2,1,4,64,512]{4,3,2,1,0:T(8,128)S(1)}, f32[2,1,4,64,512]{4,3,2,1,0:T(8,128)}, u32[]{:S(2)}) %copy-start) | copy-done | bytes 1048600
  9.3 1.6 %collective-permute-start = (f32[4,48,512]{2,1,0:T(8,128)S(1)}, f32[4,48,512]{2,1,0:T(8,128)S(1)}, u32[]{:S(2)}, u32[]{:S(2)}) collective-permute-start(f32[4,48,512]{2,1,0:T(8,128)S(1)} %get-tuple-element.23.refs_1_), channel_id=1, source_target_pairs={{0,2},{1,3},{2,0},{3,1},{4,6},{5,7},{6,4},{7,5},{8,10},{9,11},{10,... | collective-permute-start | bytes 1179656 | tf_op jit(solution)/shard_map/ppermute | solution.py:550
  10.9 0.1 collective-permute-start.5
  11.0 1.2 %collective-permute-start.2 = (f32[120,512]{1,0:T(8,128)S(1)}, f32[120,512]{1,0:T(8,128)S(1)}, u32[]{:S(2)}, u32[]{:S(2)}) collective-permute-start(f32[120,512]{1,0:T(8,128)S(1)} %get-tuple-element.25), channel_id=1, source_target_pairs={{0,1},{1,0},{2,3},{3,2},{4,5},{5,4},{6,7},{7,6},{8,9},{9,8},{10,11... | collective-permute-start | bytes 737288 | tf_op jit(solution)/shard_map/ppermute | solution.py:550
  12.2 0.0 collective-permute-done.4.refs_1_.refs_0_
  12.2 2.3 %collective-permute-start.7 = (f32[64,768]{1,0:T(8,128)S(1)}, f32[64,768]{1,0:T(8,128)S(1)}, u32[]{:S(2)}, u32[]{:S(2)}) collective-permute-start(f32[64,768]{1,0:T(8,128)S(1)} %pack_kernel.7), channel_id=1, source_target_pairs={{0,8},{4,12},{8,0},{12,4},{16,24},{20,28},{24,16},{28,20},{1,9},{5... | collective-permute-start | bytes 589832 | tf_op jit(solution)/shard_map/ppermute | solution.py:550
  14.5 0.0 collective-permute-done.3.refs_2_.refs_0_
  14.5 0.0 copy-start.1
  14.5 0.0 copy-start.2
  14.5 3.0 %collective-permute-start.8 = (f32[32,768]{1,0:T(8,128)S(1)}, f32[32,768]{1,0:T(8,128)S(1)}, u32[]{:S(2)}, u32[]{:S(2)}) collective-permute-start(f32[32,768]{1,0:T(8,128)S(1)} %pack_kernel.8), channel_id=1, source_target_pairs={{0,8},{4,12},{8,0},{12,4},{16,24},{20,28},{24,16},{28,20},{1,9},{5... | collective-permute-start | bytes 294920 | tf_op jit(solution)/shard_map/ppermute | solution.py:550
  17.5 0.0 collective-permute-done.5.refs_3_
  17.6 1.2 %collective-permute-start.1 = (f32[8,512]{1,0:T(8,128)S(1)}, f32[8,512]{1,0:T(8,128)S(1)}, u32[]{:S(2)}, u32[]{:S(2)}) collective-permute-start(f32[8,512]{1,0:T(8,128)S(1)} %get-tuple-element.24), channel_id=1, source_target_pairs={{0,3},{1,2},{2,1},{3,0},{4,7},{5,6},{6,5},{7,4},{8,11},{9,10},{10,... | collective-permute-start | bytes 49160 | tf_op jit(solution)/shard_map/ppermute | solution.py:550
  18.8 0.0 copy-done.1
  18.8 0.0 copy-done.2
  18.8 0.0 copy-start.5
  18.9 0.8 %own_rows_kernel.1 = (f32[2,6,64,128]{3,2,1,0:T(8,128)S(1)}, f32[2,6,64,128]{3,2,1,0:T(8,128)S(1)}) custom-call(f32[2,1,4,64,512]{4,3,2,1,0:T(8,128)S(1)} %copy-done.1, bf16[4,256,512]{2,1,0:T(8,128)(2,1)S(1)} %copy-done.2, f32[32,768]{1,0:T(8,128)S(1)} %collective-permute-done.3.refs_2_.refs_0_), custom_call_target="tpu_custom_call" | custom-call | bytes 2883584 | tf_op jit(solution)/shard_map/own_rows_kernel/pallas_call | solution.py:533
  19.7 2.7 %collective-permute-done.8.refs_1_ = f32[32,768]{1,0:T(8,128)S(1)} collective-permute-done((f32[32,768]{1,0:T(8,128)S(1)}, f32[32,768]{1,0:T(8,128)S(1)}, u32[]{:S(2)}, u32[]{:S(2)}) %collective-permute-start.8) | collective-permute-done | bytes 98336 | tf_op jit(solution)/shard_map/ppermute | solution.py:550
  22.4 0.0 collective-permute-start.6
  22.4 0.0 collective-permute-done.2.refs_2_
  22.4 0.0 collective-permute-done.7.refs_0_
  22.5 0.6 %collective-permute-start.9 = (f32[128,768]{1,0:T(8,128)S(1)}, f32[128,768]{1,0:T(8,128)S(1)}, u32[]{:S(2)}, u32[]{:S(2)}) collective-permute-start(f32[128,768]{1,0:T(8,128)S(1)} %pack_kernel.9.refs_4_), channel_id=1, source_target_pairs={{0,4},{4,0},{8,12},{12,8},{16,20},{20,16},{24,28},{28,24},{1,5},{5... | collective-permute-start | bytes 1179656 | tf_op jit(solution)/shard_map/ppermute | solution.py:550
  23.0 0.0 collective-permute-done.1.refs_1_
  23.0 0.0 collective-permute-done.refs_0_
  23.0 0.0 copy-done.5
  23.0 2.3 %inverse_kernel.1 = (f32[256,768]{1,0:T(8,128)S(1)}, f32[256,768]{1,0:T(8,128)S(1)}) custom-call(f32[4,48,512]{2,1,0:T(8,128)S(1)} %collective-permute-done.refs_0_, f32[8,512]{1,0:T(8,128)S(1)} %collective-permute-done.1.refs_1_, f32[120,512]{1,0:T(8,128)S(1)} %collective-permute-done.2.refs_2_, f32[2,6,64,128]{3,2,1,0:T(8,128)S(1)} %get-tuple-element.26.refs_3_, ...), custom_call_target="tpu_custom_call" | custom-call | flops 10000000000 | bytes 5111808 | tf_op jit(solution)/shard_map/inverse_kernel/pallas_call | solution.py:533
  25.4 0.0 collective-permute-done.6.refs_3_
  25.4 0.0 collective-permute-done.9.refs_5_
  25.4 0.5 %advection_kernel.3 = (f32[128,256]{1,0:T(8,128)S(1)}, f32[128,256]{1,0:T(8,128)S(1)}, f32[128,256]{1,0:T(8,128)S(1)}, f32[128,256]{1,0:T(8,128)S(1)}) custom-call(f32[256,768]{1,0:T(8,128)S(1)} %get-tuple-element.28.refs_0_, f32[256,768]{1,0:T(8,128)S(1)} %get-tuple-element.29.refs_1_, f32[128,768]{1,0:T(8,128)S(1)} %pack_kernel.6.refs_2_, ...), custom_call_target="tpu_custom_call" | custom-call | bytes 4718592 | tf_op jit(solution)/shard_map/advection_kernel/pallas_call | solution.py:533
  25.9 0.8 %collective-permute-start.13 = (f32[128,256]{1,0:T(8,128)S(1)}, f32[128,256]{1,0:T(8,128)S(1)}, u32[]{:S(2)}, u32[]{:S(2)}) collective-permute-start(f32[128,256]{1,0:T(8,128)S(1)} %get-tuple-element.35), channel_id=1, source_target_pairs={{0,1},{1,0},{2,3},{3,2},{4,5},{5,4},{6,7},{7,6},{8,9},{9,8},{10,11... | collective-permute-start | bytes 393224 | tf_op jit(solution)/shard_map/ppermute | solution.py:550
  26.7 1.3 %collective-permute-start.14 = (f32[128,256]{1,0:T(8,128)S(1)}, f32[128,256]{1,0:T(8,128)S(1)}, u32[]{:S(2)}, u32[]{:S(2)}) collective-permute-start(f32[128,256]{1,0:T(8,128)S(1)} %get-tuple-element.36), channel_id=1, source_target_pairs={{0,2},{1,3},{2,0},{3,1},{4,6},{5,7},{6,4},{7,5},{8,10},{9,11},{10,... | collective-permute-start | bytes 393224 | tf_op jit(solution)/shard_map/ppermute | solution.py:550
  28.0 0.0 copy-start.3
  28.0 1.4 %collective-permute-start.15 = (f32[128,256]{1,0:T(8,128)S(1)}, f32[128,256]{1,0:T(8,128)S(1)}, u32[]{:S(2)}, u32[]{:S(2)}) collective-permute-start(f32[128,256]{1,0:T(8,128)S(1)} %get-tuple-element.37), channel_id=1, source_target_pairs={{0,3},{1,2},{2,1},{3,0},{4,7},{5,6},{6,5},{7,4},{8,11},{9,10},{10,... | collective-permute-start | bytes 393224 | tf_op jit(solution)/shard_map/ppermute | solution.py:550
  29.4 0.5 %advection_kernel.2 = (f32[128,256]{1,0:T(8,128)S(1)}, f32[128,256]{1,0:T(8,128)S(1)}, f32[128,256]{1,0:T(8,128)S(1)}, f32[128,256]{1,0:T(8,128)S(1)}) custom-call(f32[256,768]{1,0:T(8,128)S(1)} %get-tuple-element.28.refs_0_, f32[256,768]{1,0:T(8,128)S(1)} %get-tuple-element.29.refs_1_, f32[128,768]{1,0:T(8,128)S(1)} %pack_kernel.6.refs_2_, ...), custom_call_target="tpu_custom_call" | custom-call | bytes 4718592 | tf_op jit(solution)/shard_map/advection_kernel/pallas_call | solution.py:533
  29.9 0.8 %collective-permute-start.10 = (f32[128,256]{1,0:T(8,128)S(1)}, f32[128,256]{1,0:T(8,128)S(1)}, u32[]{:S(2)}, u32[]{:S(2)}) collective-permute-start(f32[128,256]{1,0:T(8,128)S(1)} %get-tuple-element.31), channel_id=1, source_target_pairs={{0,1},{1,0},{2,3},{3,2},{4,5},{5,4},{6,7},{7,6},{8,9},{9,8},{10,11... | collective-permute-start | bytes 393224 | tf_op jit(solution)/shard_map/ppermute | solution.py:550
  30.7 1.3 %collective-permute-start.11 = (f32[128,256]{1,0:T(8,128)S(1)}, f32[128,256]{1,0:T(8,128)S(1)}, u32[]{:S(2)}, u32[]{:S(2)}) collective-permute-start(f32[128,256]{1,0:T(8,128)S(1)} %get-tuple-element.32), channel_id=1, source_target_pairs={{0,2},{1,3},{2,0},{3,1},{4,6},{5,7},{6,4},{7,5},{8,10},{9,11},{10,... | collective-permute-start | bytes 393224 | tf_op jit(solution)/shard_map/ppermute | solution.py:550
  32.0 0.3 collective-permute-done.13.refs_1_
  32.3 1.2 %collective-permute-start.12 = (f32[128,256]{1,0:T(8,128)S(1)}, f32[128,256]{1,0:T(8,128)S(1)}, u32[]{:S(2)}, u32[]{:S(2)}) collective-permute-start(f32[128,256]{1,0:T(8,128)S(1)} %get-tuple-element.33), channel_id=1, source_target_pairs={{0,3},{1,2},{2,1},{3,0},{4,7},{5,6},{6,5},{7,4},{8,11},{9,10},{10,... | collective-permute-start | bytes 393224 | tf_op jit(solution)/shard_map/ppermute | solution.py:550
  33.5 0.0 copy-done.3
  33.5 0.4 %linear_kernel.1.refs_5_ = f32[2,1,4,64,512]{4,3,2,1,0:T(8,128)S(1)} custom-call(f32[2,1,4,64,512]{4,3,2,1,0:T(8,128)S(1)} %copy-done.1, f32[2,1,4,64,512]{4,3,2,1,0:T(8,128)S(1)} %copy-done.3, f32[128,256]{1,0:T(8,128)S(1)} %get-tuple-element.30.refs_2_.refs_0_), custom_call_target="tpu_custom_call" | custom-call | bytes 3145728 | tf_op jit(solution)/shard_map/linear_kernel/pallas_call | solution.py:533
  33.9 0.0 collective-permute-done.14.refs_2_
  33.9 2.0 %collective-permute-done.15.refs_3_ = f32[128,256]{1,0:T(8,128)S(1)} collective-permute-done((f32[128,256]{1,0:T(8,128)S(1)}, f32[128,256]{1,0:T(8,128)S(1)}, u32[]{:S(2)}, u32[]{:S(2)}) %collective-permute-start.15) | collective-permute-done | bytes 131104 | tf_op jit(solution)/shard_map/ppermute | solution.py:550
  35.9 1.7 %final_kernel.2 = (f32[2,1,4,64,512]{4,3,2,1,0:T(8,128)}, f32[2,1,4,64,512]{4,3,2,1,0:T(8,128)}) custom-call(f32[128,256]{1,0:T(8,128)S(1)} %get-tuple-element.34.refs_0_, f32[128,256]{1,0:T(8,128)S(1)} %collective-permute-done.13.refs_1_, f32[128,256]{1,0:T(8,128)S(1)} %collective-permute-done.14.refs_2_, f32[128,256]{1,0:T(8,128)S(1)} %collective-permute-done.15.refs_3_, ...), custom_call_target="tpu_custom_call" | custom-call | bytes 5767168 | tf_op jit(solution)/shard_map/final_kernel/pallas_call | solution.py:533
  37.6 0.3 collective-permute-done.10.refs_1_
  38.0 1.2 %collective-permute-done.11.refs_2_ = f32[128,256]{1,0:T(8,128)S(1)} collective-permute-done((f32[128,256]{1,0:T(8,128)S(1)}, f32[128,256]{1,0:T(8,128)S(1)}, u32[]{:S(2)}, u32[]{:S(2)}) %collective-permute-start.11) | collective-permute-done | bytes 131104 | tf_op jit(solution)/shard_map/ppermute | solution.py:550
  39.1 1.5 %collective-permute-done.12.refs_3_ = f32[128,256]{1,0:T(8,128)S(1)} collective-permute-done((f32[128,256]{1,0:T(8,128)S(1)}, f32[128,256]{1,0:T(8,128)S(1)}, u32[]{:S(2)}, u32[]{:S(2)}) %collective-permute-start.12) | collective-permute-done | bytes 131104 | tf_op jit(solution)/shard_map/ppermute | solution.py:550
  40.6 1.7 %final_kernel.3 = (f32[2,1,4,64,512]{4,3,2,1,0:T(8,128)}, f32[2,1,4,64,512]{4,3,2,1,0:T(8,128)}) custom-call(f32[128,256]{1,0:T(8,128)S(1)} %get-tuple-element.30.refs_2_.refs_0_, f32[128,256]{1,0:T(8,128)S(1)} %collective-permute-done.10.refs_1_, f32[128,256]{1,0:T(8,128)S(1)} %collective-permute-done.11.refs_2_, ...), custom_call_target="tpu_custom_call", output_to_operand_aliasing={{0}: (7, {}), {1}: (8, {})} | custom-call | bytes 5767168 | tf_op jit(solution)/shard_map/final_kernel/pallas_call | solution.py:533
  (6 shorter events, 0.1 us)
Async XLA Ops:
  0.6 1.0 %copy-start.4 = (f32[6,4,64,32]{2,3,1,0:T(8,128)S(1)}, f32[6,4,64,32]{2,3,1,0:T(8,128)}, u32[]{:S(2)}) copy-start(f32[6,4,64,32]{2,3,1,0:T(8,128)} %param.7) | copy-start | bytes 589828
  1.7 10.4 %collective-permute-start.4 = (f32[32,768]{1,0:T(8,128)S(1)}, f32[32,768]{1,0:T(8,128)S(1)}, u32[]{:S(2)}, u32[]{:S(2)}) collective-permute-start(f32[32,768]{1,0:T(8,128)S(1)} %get-tuple-element.22.refs_2_.refs_0_.refs_1_), channel_id=1, source_target_pairs={{0,24},{4,28},{8,16},{12,20},{16,8},{20,12},{24,0},{28,4},{1,25},{... | collective-permute-start | bytes 294920 | tf_op jit(solution)/shard_map/ppermute | solution.py:550
  6.9 7.7 %collective-permute-start.3 = (f32[32,768]{1,0:T(8,128)S(1)}, f32[32,768]{1,0:T(8,128)S(1)}, u32[]{:S(2)}, u32[]{:S(2)}) collective-permute-start(f32[32,768]{1,0:T(8,128)S(1)} %get-tuple-element.21.refs_0_), channel_id=1, source_target_pairs={{0,25},{1,24},{2,27},{3,26},{4,29},{5,28},{6,31},{7,30},{8,17},{9,... | collective-permute-start | bytes 294920 | tf_op jit(solution)/shard_map/ppermute | solution.py:550
  8.0 1.2 %copy-start = (f32[2,1,4,64,512]{4,3,2,1,0:T(8,128)S(1)}, f32[2,1,4,64,512]{4,3,2,1,0:T(8,128)}, u32[]{:S(2)}) copy-start(f32[2,1,4,64,512]{4,3,2,1,0:T(8,128)} %refs_4_.3) | copy-start | bytes 3145732
  9.3 13.7 %collective-permute-start = (f32[4,48,512]{2,1,0:T(8,128)S(1)}, f32[4,48,512]{2,1,0:T(8,128)S(1)}, u32[]{:S(2)}, u32[]{:S(2)}) collective-permute-start(f32[4,48,512]{2,1,0:T(8,128)S(1)} %get-tuple-element.23.refs_1_), channel_id=1, source_target_pairs={{0,2},{1,3},{2,0},{3,1},{4,6},{5,7},{6,4},{7,5},{8,10},{9,11},{10,... | collective-permute-start | bytes 1179656 | tf_op jit(solution)/shard_map/ppermute | solution.py:550
  10.9 6.7 %collective-permute-start.5 = (f32[32,768]{1,0:T(8,128)S(1)}, f32[32,768]{1,0:T(8,128)S(1)}, u32[]{:S(2)}, u32[]{:S(2)}) collective-permute-start(f32[32,768]{1,0:T(8,128)S(1)} %pack_kernel.5), channel_id=1, source_target_pairs={{0,9},{1,8},{2,11},{3,10},{4,13},{5,12},{6,15},{7,14},{8,1},{9,0},... | collective-permute-start | bytes 294920 | tf_op jit(solution)/shard_map/ppermute | solution.py:550
  11.0 11.5 %collective-permute-start.2 = (f32[120,512]{1,0:T(8,128)S(1)}, f32[120,512]{1,0:T(8,128)S(1)}, u32[]{:S(2)}, u32[]{:S(2)}) collective-permute-start(f32[120,512]{1,0:T(8,128)S(1)} %get-tuple-element.25), channel_id=1, source_target_pairs={{0,1},{1,0},{2,3},{3,2},{4,5},{5,4},{6,7},{7,6},{8,9},{9,8},{10,11... | collective-permute-start | bytes 737288 | tf_op jit(solution)/shard_map/ppermute | solution.py:550
  12.2 10.2 %collective-permute-start.7 = (f32[64,768]{1,0:T(8,128)S(1)}, f32[64,768]{1,0:T(8,128)S(1)}, u32[]{:S(2)}, u32[]{:S(2)}) collective-permute-start(f32[64,768]{1,0:T(8,128)S(1)} %pack_kernel.7), channel_id=1, source_target_pairs={{0,8},{4,12},{8,0},{12,4},{16,24},{20,28},{24,16},{28,20},{1,9},{5... | collective-permute-start | bytes 589832 | tf_op jit(solution)/shard_map/ppermute | solution.py:550
  14.5 4.3 %copy-start.1 = (f32[2,1,4,64,512]{4,3,2,1,0:T(8,128)S(1)}, f32[2,1,4,64,512]{4,3,2,1,0:T(8,128)}, u32[]{:S(2)}) copy-start(f32[2,1,4,64,512]{4,3,2,1,0:T(8,128)} %refs_4_.3) | copy-start | bytes 3145732
  14.5 4.3 %copy-start.2 = (bf16[4,256,512]{2,1,0:T(8,128)(2,1)S(1)}, bf16[4,256,512]{2,1,0:T(8,128)(2,1)}, u32[]{:S(2)}) copy-start(bf16[4,256,512]{2,1,0:T(8,128)(2,1)} %constant.4.clone.refs_1_.refs_5_.refs_6_) | copy-start | bytes 3145732
  14.5 7.9 %collective-permute-start.8 = (f32[32,768]{1,0:T(8,128)S(1)}, f32[32,768]{1,0:T(8,128)S(1)}, u32[]{:S(2)}, u32[]{:S(2)}) collective-permute-start(f32[32,768]{1,0:T(8,128)S(1)} %pack_kernel.8), channel_id=1, source_target_pairs={{0,8},{4,12},{8,0},{12,4},{16,24},{20,28},{24,16},{28,20},{1,9},{5... | collective-permute-start | bytes 294920 | tf_op jit(solution)/shard_map/ppermute | solution.py:550
  17.6 5.5 %collective-permute-start.1 = (f32[8,512]{1,0:T(8,128)S(1)}, f32[8,512]{1,0:T(8,128)S(1)}, u32[]{:S(2)}, u32[]{:S(2)}) collective-permute-start(f32[8,512]{1,0:T(8,128)S(1)} %get-tuple-element.24), channel_id=1, source_target_pairs={{0,3},{1,2},{2,1},{3,0},{4,7},{5,6},{6,5},{7,4},{8,11},{9,10},{10,... | collective-permute-start | bytes 49160 | tf_op jit(solution)/shard_map/ppermute | solution.py:550
  18.8 4.2 %copy-start.5 = (bf16[4,2,256,256]{3,2,1,0:T(8,128)(2,1)S(1)}, bf16[4,2,256,256]{3,2,1,0:T(8,128)(2,1)}, u32[]{:S(2)}) copy-start(bf16[4,2,256,256]{3,2,1,0:T(8,128)(2,1)} %constant.5.clone.refs_6_) | copy-start | bytes 3145732
  22.4 2.9 %collective-permute-start.6 = (f32[128,768]{1,0:T(8,128)S(1)}, f32[128,768]{1,0:T(8,128)S(1)}, u32[]{:S(2)}, u32[]{:S(2)}) collective-permute-start(f32[128,768]{1,0:T(8,128)S(1)} %pack_kernel.6.refs_2_), channel_id=1, source_target_pairs={{0,4},{4,0},{8,12},{12,8},{16,20},{20,16},{24,28},{28,24},{1,5},{5... | collective-permute-start | bytes 1179656 | tf_op jit(solution)/shard_map/ppermute | solution.py:550
  22.5 2.9 %collective-permute-start.9 = (f32[128,768]{1,0:T(8,128)S(1)}, f32[128,768]{1,0:T(8,128)S(1)}, u32[]{:S(2)}, u32[]{:S(2)}) collective-permute-start(f32[128,768]{1,0:T(8,128)S(1)} %pack_kernel.9.refs_4_), channel_id=1, source_target_pairs={{0,4},{4,0},{8,12},{12,8},{16,20},{20,16},{24,28},{28,24},{1,5},{5... | collective-permute-start | bytes 1179656 | tf_op jit(solution)/shard_map/ppermute | solution.py:550
  25.9 6.4 %collective-permute-start.13 = (f32[128,256]{1,0:T(8,128)S(1)}, f32[128,256]{1,0:T(8,128)S(1)}, u32[]{:S(2)}, u32[]{:S(2)}) collective-permute-start(f32[128,256]{1,0:T(8,128)S(1)} %get-tuple-element.35), channel_id=1, source_target_pairs={{0,1},{1,0},{2,3},{3,2},{4,5},{5,4},{6,7},{7,6},{8,9},{9,8},{10,11... | collective-permute-start | bytes 393224 | tf_op jit(solution)/shard_map/ppermute | solution.py:550
  26.7 7.2 %collective-permute-start.14 = (f32[128,256]{1,0:T(8,128)S(1)}, f32[128,256]{1,0:T(8,128)S(1)}, u32[]{:S(2)}, u32[]{:S(2)}) collective-permute-start(f32[128,256]{1,0:T(8,128)S(1)} %get-tuple-element.36), channel_id=1, source_target_pairs={{0,2},{1,3},{2,0},{3,1},{4,6},{5,7},{6,4},{7,5},{8,10},{9,11},{10,... | collective-permute-start | bytes 393224 | tf_op jit(solution)/shard_map/ppermute | solution.py:550
  28.0 5.5 %copy-start.3 = (f32[2,1,4,64,512]{4,3,2,1,0:T(8,128)S(1)}, f32[2,1,4,64,512]{4,3,2,1,0:T(8,128)}, u32[]{:S(2)}) copy-start(f32[2,1,4,64,512]{4,3,2,1,0:T(8,128)} %refs_1_.4) | copy-start | bytes 3145732
  28.0 7.9 %collective-permute-start.15 = (f32[128,256]{1,0:T(8,128)S(1)}, f32[128,256]{1,0:T(8,128)S(1)}, u32[]{:S(2)}, u32[]{:S(2)}) collective-permute-start(f32[128,256]{1,0:T(8,128)S(1)} %get-tuple-element.37), channel_id=1, source_target_pairs={{0,3},{1,2},{2,1},{3,0},{4,7},{5,6},{6,5},{7,4},{8,11},{9,10},{10,... | collective-permute-start | bytes 393224 | tf_op jit(solution)/shard_map/ppermute | solution.py:550
  29.9 8.0 %collective-permute-start.10 = (f32[128,256]{1,0:T(8,128)S(1)}, f32[128,256]{1,0:T(8,128)S(1)}, u32[]{:S(2)}, u32[]{:S(2)}) collective-permute-start(f32[128,256]{1,0:T(8,128)S(1)} %get-tuple-element.31), channel_id=1, source_target_pairs={{0,1},{1,0},{2,3},{3,2},{4,5},{5,4},{6,7},{7,6},{8,9},{9,8},{10,11... | collective-permute-start | bytes 393224 | tf_op jit(solution)/shard_map/ppermute | solution.py:550
  30.7 8.4 %collective-permute-start.11 = (f32[128,256]{1,0:T(8,128)S(1)}, f32[128,256]{1,0:T(8,128)S(1)}, u32[]{:S(2)}, u32[]{:S(2)}) collective-permute-start(f32[128,256]{1,0:T(8,128)S(1)} %get-tuple-element.32), channel_id=1, source_target_pairs={{0,2},{1,3},{2,0},{3,1},{4,6},{5,7},{6,4},{7,5},{8,10},{9,11},{10,... | collective-permute-start | bytes 393224 | tf_op jit(solution)/shard_map/ppermute | solution.py:550
  32.3 8.3 %collective-permute-start.12 = (f32[128,256]{1,0:T(8,128)S(1)}, f32[128,256]{1,0:T(8,128)S(1)}, u32[]{:S(2)}, u32[]{:S(2)}) collective-permute-start(f32[128,256]{1,0:T(8,128)S(1)} %get-tuple-element.33), channel_id=1, source_target_pairs={{0,3},{1,2},{2,1},{3,0},{4,7},{5,6},{6,5},{7,4},{8,11},{9,10},{10,... | collective-permute-start | bytes 393224 | tf_op jit(solution)/shard_map/ppermute | solution.py:550

commit v2 on v1

--- a/solution.py
+++ b/solution.py
@@ -178,7 +178,7 @@
 PEN = 4
 EXTRA = 8
 NEAR_X = 16
-HINT = dict(own=0, inverse=10**10, forward=5 * 10**9, early=0, pack=0, advect=(0, 0), linear=0)
+HINT = dict(inverse=10**10, forward=5 * 10**9)
 
 
 def split(values):
@@ -598,10 +598,10 @@
         functools.partial(own_rows_kernel, grid),
         [shape((2, fields, rows, lanes))] * 2,
         [],
-        HINT["own"],
+        0,
         [state, table],
         after=[swap_far],
-            )
+    )
     own_fields, swap_fields = call(
         functools.partial(inverse_kernel, grid),
         [shape((grid, base_lanes))] * 2,
@@ -620,8 +620,8 @@
     packs = []
     for (blocks, cost, after), group in zip(
         (
-            ([own_base, own_far, swap_far, swap_near], HINT["early"], ()),
-            ([own_forward, swap_forward, came], HINT["pack"], ()),
+            ([own_base, own_far, swap_far, swap_near], 0, ()),
+            ([own_forward, swap_forward, came], 0, ()),
         ),
         places,
         strict=True,
@@ -634,7 +634,7 @@
             functools.partial(advection_kernel, places, field),
             [shape((2 * rows, 2 * lanes))] * PEN,
             [pltpu.VMEM((grid, 2 * lanes), bf16)] * 2,
-            HINT["advect"][field],
+            0,
             [own_fields, swap_fields, *packs, table],
         )
         made.append(messages[0])
@@ -645,7 +645,7 @@
         functools.partial(linear_kernel, grid),
         [shape(state.shape)],
         [],
-        HINT["linear"],
+        0,
         [state, accum],
         after=made[1:],
     )

time: 42.5 us -> 42.5 us (level)
  no operation moved by 1% of the time
where the time goes in v2:
time: 42.5 us; the launch traced here: 42.3 us
  starting transfers between devices  23.1 us (54%)
  Pallas kernels  8.19 us (19%)
  waiting for transfers between devices  8.02 us (19%)
  local copies, waits for them, and re-layouts  2.23 us (5%)
  between operations  0.78 us (2%)
    ppermute x16, starting transfers between devices, exchange(): lax.ppermute(values, axis, [(index, index ^ mask) for index in range(size)])  23.1 us
    pallas_call x14, Pallas kernels, call(): pl.pallas_call(lambda *refs: kernel(*refs[:count], *refs[total:]), out_sh...  8.19 us
    ppermute x16, waiting for transfers between devices, exchange(): lax.ppermute(values, axis, [(index, index ^ mask) for index in range(size)])  8.02 us
    unnamed x12, local copies, waits for them, and re-layouts  2.23 us
  transfers between devices with their start and end apart: 16, of which 6 were waited for; matrix products, arithmetic and copies ran while one was open for 0% of the time, Pallas kernels for 14%

profile of v2, /device:TPU:0, one launch (start us, length us, event | category | flops | bytes accessed | tf_op | source)
XLA Modules:
  0.0 42.3 jit_solution(8768876224513607438)
XLA Ops:
  0.6 0.0 copy-start.4
  0.6 1.0 %copy-done.4 = f32[6,4,64,32]{2,3,1,0:T(8,128)S(1)} copy-done((f32[6,4,64,32]{2,3,1,0:T(8,128)S(1)}, f32[6,4,64,32]{2,3,1,0:T(8,128)}, u32[]{:S(2)}) %copy-start.4) | copy-done | bytes 196632
  1.6 0.1 base_kernel.1
  1.7 5.1 %collective-permute-start.4 = (f32[32,768]{1,0:T(8,128)S(1)}, f32[32,768]{1,0:T(8,128)S(1)}, u32[]{:S(2)}, u32[]{:S(2)}) collective-permute-start(f32[32,768]{1,0:T(8,128)S(1)} %get-tuple-element.22.refs_2_.refs_0_.refs_1_), channel_id=1, source_target_pairs={{0,24},{4,28},{8,16},{12,20},{16,8},{20,12},{24,0},{28,4},{1,25},{... | collective-permute-start | bytes 294920 | tf_op jit(solution)/shard_map/ppermute | solution.py:550
  6.9 1.1 %collective-permute-start.3 = (f32[32,768]{1,0:T(8,128)S(1)}, f32[32,768]{1,0:T(8,128)S(1)}, u32[]{:S(2)}, u32[]{:S(2)}) collective-permute-start(f32[32,768]{1,0:T(8,128)S(1)} %get-tuple-element.21.refs_0_), channel_id=1, source_target_pairs={{0,25},{1,24},{2,27},{3,26},{4,29},{5,28},{6,31},{7,30},{8,17},{9,... | collective-permute-start | bytes 294920 | tf_op jit(solution)/shard_map/ppermute | solution.py:550
  8.0 0.0 copy-start
  8.0 1.2 %copy-done = f32[2,1,4,64,512]{4,3,2,1,0:T(8,128)S(1)} copy-done((f32[2,1,4,64,512]{4,3,2,1,0:T(8,128)S(1)}, f32[2,1,4,64,512]{4,3,2,1,0:T(8,128)}, u32[]{:S(2)}) %copy-start) | copy-done | bytes 1048600
  9.3 1.6 %collective-permute-start = (f32[4,48,512]{2,1,0:T(8,128)S(1)}, f32[4,48,512]{2,1,0:T(8,128)S(1)}, u32[]{:S(2)}, u32[]{:S(2)}) collective-permute-start(f32[4,48,512]{2,1,0:T(8,128)S(1)} %get-tuple-element.23.refs_1_), channel_id=1, source_target_pairs={{0,2},{1,3},{2,0},{3,1},{4,6},{5,7},{6,4},{7,5},{8,10},{9,11},{10,... | collective-permute-start | bytes 1179656 | tf_op jit(solution)/shard_map/ppermute | solution.py:550
  10.9 0.1 collective-permute-start.5
  11.0 1.2 %collective-permute-start.2 = (f32[120,512]{1,0:T(8,128)S(1)}, f32[120,512]{1,0:T(8,128)S(1)}, u32[]{:S(2)}, u32[]{:S(2)}) collective-permute-start(f32[120,512]{1,0:T(8,128)S(1)} %get-tuple-element.25), channel_id=1, source_target_pairs={{0,1},{1,0},{2,3},{3,2},{4,5},{5,4},{6,7},{7,6},{8,9},{9,8},{10,11... | collective-permute-start | bytes 737288 | tf_op jit(solution)/shard_map/ppermute | solution.py:550
  12.2 0.0 collective-permute-done.4.refs_1_.refs_0_
  12.2 2.3 %collective-permute-start.7 = (f32[64,768]{1,0:T(8,128)S(1)}, f32[64,768]{1,0:T(8,128)S(1)}, u32[]{:S(2)}, u32[]{:S(2)}) collective-permute-start(f32[64,768]{1,0:T(8,128)S(1)} %pack_kernel.7), channel_id=1, source_target_pairs={{0,8},{4,12},{8,0},{12,4},{16,24},{20,28},{24,16},{28,20},{1,9},{5... | collective-permute-start | bytes 589832 | tf_op jit(solution)/shard_map/ppermute | solution.py:550
  14.5 0.0 collective-permute-done.3.refs_2_.refs_0_
  14.5 0.0 copy-start.1
  14.5 0.0 copy-start.2
  14.5 3.0 %collective-permute-start.8 = (f32[32,768]{1,0:T(8,128)S(1)}, f32[32,768]{1,0:T(8,128)S(1)}, u32[]{:S(2)}, u32[]{:S(2)}) collective-permute-start(f32[32,768]{1,0:T(8,128)S(1)} %pack_kernel.8), channel_id=1, source_target_pairs={{0,8},{4,12},{8,0},{12,4},{16,24},{20,28},{24,16},{28,20},{1,9},{5... | collective-permute-start | bytes 294920 | tf_op jit(solution)/shard_map/ppermute | solution.py:550
  17.5 0.0 collective-permute-done.5.refs_3_
  17.6 1.2 %collective-permute-start.1 = (f32[8,512]{1,0:T(8,128)S(1)}, f32[8,512]{1,0:T(8,128)S(1)}, u32[]{:S(2)}, u32[]{:S(2)}) collective-permute-start(f32[8,512]{1,0:T(8,128)S(1)} %get-tuple-element.24), channel_id=1, source_target_pairs={{0,3},{1,2},{2,1},{3,0},{4,7},{5,6},{6,5},{7,4},{8,11},{9,10},{10,... | collective-permute-start | bytes 49160 | tf_op jit(solution)/shard_map/ppermute | solution.py:550
  18.8 0.0 copy-done.1
  18.8 0.0 copy-done.2
  18.8 0.0 copy-start.5
  18.9 0.8 %own_rows_kernel.1 = (f32[2,6,64,128]{3,2,1,0:T(8,128)S(1)}, f32[2,6,64,128]{3,2,1,0:T(8,128)S(1)}) custom-call(f32[2,1,4,64,512]{4,3,2,1,0:T(8,128)S(1)} %copy-done.1, bf16[4,256,512]{2,1,0:T(8,128)(2,1)S(1)} %copy-done.2, f32[32,768]{1,0:T(8,128)S(1)} %collective-permute-done.3.refs_2_.refs_0_), custom_call_target="tpu_custom_call" | custom-call | bytes 2883584 | tf_op jit(solution)/shard_map/own_rows_kernel/pallas_call | solution.py:533
  19.7 2.7 %collective-permute-done.8.refs_1_ = f32[32,768]{1,0:T(8,128)S(1)} collective-permute-done((f32[32,768]{1,0:T(8,128)S(1)}, f32[32,768]{1,0:T(8,128)S(1)}, u32[]{:S(2)}, u32[]{:S(2)}) %collective-permute-start.8) | collective-permute-done | bytes 98336 | tf_op jit(solution)/shard_map/ppermute | solution.py:550
  22.4 0.0 collective-permute-start.6
  22.4 0.0 collective-permute-done.2.refs_2_
  22.4 0.0 collective-permute-done.7.refs_0_
  22.5 0.6 %collective-permute-start.9 = (f32[128,768]{1,0:T(8,128)S(1)}, f32[128,768]{1,0:T(8,128)S(1)}, u32[]{:S(2)}, u32[]{:S(2)}) collective-permute-start(f32[128,768]{1,0:T(8,128)S(1)} %pack_kernel.9.refs_4_), channel_id=1, source_target_pairs={{0,4},{4,0},{8,12},{12,8},{16,20},{20,16},{24,28},{28,24},{1,5},{5... | collective-permute-start | bytes 1179656 | tf_op jit(solution)/shard_map/ppermute | solution.py:550
  23.0 0.0 collective-permute-done.1.refs_1_
  23.0 0.0 collective-permute-done.refs_0_
  23.0 0.0 copy-done.5
  23.0 2.3 %inverse_kernel.1 = (f32[256,768]{1,0:T(8,128)S(1)}, f32[256,768]{1,0:T(8,128)S(1)}) custom-call(f32[4,48,512]{2,1,0:T(8,128)S(1)} %collective-permute-done.refs_0_, f32[8,512]{1,0:T(8,128)S(1)} %collective-permute-done.1.refs_1_, f32[120,512]{1,0:T(8,128)S(1)} %collective-permute-done.2.refs_2_, f32[2,6,64,128]{3,2,1,0:T(8,128)S(1)} %get-tuple-element.26.refs_3_, ...), custom_call_target="tpu_custom_call" | custom-call | flops 10000000000 | bytes 5111808 | tf_op jit(solution)/shard_map/inverse_kernel/pallas_call | solution.py:533
  25.4 0.0 collective-permute-done.6.refs_3_
  25.4 0.0 collective-permute-done.9.refs_5_
  25.4 0.5 %advection_kernel.3 = (f32[128,256]{1,0:T(8,128)S(1)}, f32[128,256]{1,0:T(8,128)S(1)}, f32[128,256]{1,0:T(8,128)S(1)}, f32[128,256]{1,0:T(8,128)S(1)}) custom-call(f32[256,768]{1,0:T(8,128)S(1)} %get-tuple-element.28.refs_0_, f32[256,768]{1,0:T(8,128)S(1)} %get-tuple-element.29.refs_1_, f32[128,768]{1,0:T(8,128)S(1)} %pack_kernel.6.refs_2_, ...), custom_call_target="tpu_custom_call" | custom-call | bytes 4718592 | tf_op jit(solution)/shard_map/advection_kernel/pallas_call | solution.py:533
  25.9 0.8 %collective-permute-start.13 = (f32[128,256]{1,0:T(8,128)S(1)}, f32[128,256]{1,0:T(8,128)S(1)}, u32[]{:S(2)}, u32[]{:S(2)}) collective-permute-start(f32[128,256]{1,0:T(8,128)S(1)} %get-tuple-element.35), channel_id=1, source_target_pairs={{0,1},{1,0},{2,3},{3,2},{4,5},{5,4},{6,7},{7,6},{8,9},{9,8},{10,11... | collective-permute-start | bytes 393224 | tf_op jit(solution)/shard_map/ppermute | solution.py:550
  26.7 1.3 %collective-permute-start.14 = (f32[128,256]{1,0:T(8,128)S(1)}, f32[128,256]{1,0:T(8,128)S(1)}, u32[]{:S(2)}, u32[]{:S(2)}) collective-permute-start(f32[128,256]{1,0:T(8,128)S(1)} %get-tuple-element.36), channel_id=1, source_target_pairs={{0,2},{1,3},{2,0},{3,1},{4,6},{5,7},{6,4},{7,5},{8,10},{9,11},{10,... | collective-permute-start | bytes 393224 | tf_op jit(solution)/shard_map/ppermute | solution.py:550
  28.0 0.0 copy-start.3
  28.0 1.4 %collective-permute-start.15 = (f32[128,256]{1,0:T(8,128)S(1)}, f32[128,256]{1,0:T(8,128)S(1)}, u32[]{:S(2)}, u32[]{:S(2)}) collective-permute-start(f32[128,256]{1,0:T(8,128)S(1)} %get-tuple-element.37), channel_id=1, source_target_pairs={{0,3},{1,2},{2,1},{3,0},{4,7},{5,6},{6,5},{7,4},{8,11},{9,10},{10,... | collective-permute-start | bytes 393224 | tf_op jit(solution)/shard_map/ppermute | solution.py:550
  29.4 0.5 %advection_kernel.2 = (f32[128,256]{1,0:T(8,128)S(1)}, f32[128,256]{1,0:T(8,128)S(1)}, f32[128,256]{1,0:T(8,128)S(1)}, f32[128,256]{1,0:T(8,128)S(1)}) custom-call(f32[256,768]{1,0:T(8,128)S(1)} %get-tuple-element.28.refs_0_, f32[256,768]{1,0:T(8,128)S(1)} %get-tuple-element.29.refs_1_, f32[128,768]{1,0:T(8,128)S(1)} %pack_kernel.6.refs_2_, ...), custom_call_target="tpu_custom_call" | custom-call | bytes 4718592 | tf_op jit(solution)/shard_map/advection_kernel/pallas_call | solution.py:533
  29.9 0.8 %collective-permute-start.10 = (f32[128,256]{1,0:T(8,128)S(1)}, f32[128,256]{1,0:T(8,128)S(1)}, u32[]{:S(2)}, u32[]{:S(2)}) collective-permute-start(f32[128,256]{1,0:T(8,128)S(1)} %get-tuple-element.31), channel_id=1, source_target_pairs={{0,1},{1,0},{2,3},{3,2},{4,5},{5,4},{6,7},{7,6},{8,9},{9,8},{10,11... | collective-permute-start | bytes 393224 | tf_op jit(solution)/shard_map/ppermute | solution.py:550
  30.7 1.3 %collective-permute-start.11 = (f32[128,256]{1,0:T(8,128)S(1)}, f32[128,256]{1,0:T(8,128)S(1)}, u32[]{:S(2)}, u32[]{:S(2)}) collective-permute-start(f32[128,256]{1,0:T(8,128)S(1)} %get-tuple-element.32), channel_id=1, source_target_pairs={{0,2},{1,3},{2,0},{3,1},{4,6},{5,7},{6,4},{7,5},{8,10},{9,11},{10,... | collective-permute-start | bytes 393224 | tf_op jit(solution)/shard_map/ppermute | solution.py:550
  32.0 0.3 collective-permute-done.13.refs_1_
  32.3 1.2 %collective-permute-start.12 = (f32[128,256]{1,0:T(8,128)S(1)}, f32[128,256]{1,0:T(8,128)S(1)}, u32[]{:S(2)}, u32[]{:S(2)}) collective-permute-start(f32[128,256]{1,0:T(8,128)S(1)} %get-tuple-element.33), channel_id=1, source_target_pairs={{0,3},{1,2},{2,1},{3,0},{4,7},{5,6},{6,5},{7,4},{8,11},{9,10},{10,... | collective-permute-start | bytes 393224 | tf_op jit(solution)/shard_map/ppermute | solution.py:550
  33.5 0.0 copy-done.3
  33.5 0.4 %linear_kernel.1.refs_5_ = f32[2,1,4,64,512]{4,3,2,1,0:T(8,128)S(1)} custom-call(f32[2,1,4,64,512]{4,3,2,1,0:T(8,128)S(1)} %copy-done.1, f32[2,1,4,64,512]{4,3,2,1,0:T(8,128)S(1)} %copy-done.3, f32[128,256]{1,0:T(8,128)S(1)} %get-tuple-element.30.refs_2_.refs_0_), custom_call_target="tpu_custom_call" | custom-call | bytes 3145728 | tf_op jit(solution)/shard_map/linear_kernel/pallas_call | solution.py:533
  33.9 0.0 collective-permute-done.14.refs_2_
  33.9 2.0 %collective-permute-done.15.refs_3_ = f32[128,256]{1,0:T(8,128)S(1)} collective-permute-done((f32[128,256]{1,0:T(8,128)S(1)}, f32[128,256]{1,0:T(8,128)S(1)}, u32[]{:S(2)}, u32[]{:S(2)}) %collective-permute-start.15) | collective-permute-done | bytes 131104 | tf_op jit(solution)/shard_map/ppermute | solution.py:550
  35.9 1.7 %final_kernel.2 = (f32[2,1,4,64,512]{4,3,2,1,0:T(8,128)}, f32[2,1,4,64,512]{4,3,2,1,0:T(8,128)}) custom-call(f32[128,256]{1,0:T(8,128)S(1)} %get-tuple-element.34.refs_0_, f32[128,256]{1,0:T(8,128)S(1)} %collective-permute-done.13.refs_1_, f32[128,256]{1,0:T(8,128)S(1)} %collective-permute-done.14.refs_2_, f32[128,256]{1,0:T(8,128)S(1)} %collective-permute-done.15.refs_3_, ...), custom_call_target="tpu_custom_call" | custom-call | bytes 5767168 | tf_op jit(solution)/shard_map/final_kernel/pallas_call | solution.py:533
  37.6 0.3 collective-permute-done.10.refs_1_
  38.0 1.2 %collective-permute-done.11.refs_2_ = f32[128,256]{1,0:T(8,128)S(1)} collective-permute-done((f32[128,256]{1,0:T(8,128)S(1)}, f32[128,256]{1,0:T(8,128)S(1)}, u32[]{:S(2)}, u32[]{:S(2)}) %collective-permute-start.11) | collective-permute-done | bytes 131104 | tf_op jit(solution)/shard_map/ppermute | solution.py:550
  39.1 1.5 %collective-permute-done.12.refs_3_ = f32[128,256]{1,0:T(8,128)S(1)} collective-permute-done((f32[128,256]{1,0:T(8,128)S(1)}, f32[128,256]{1,0:T(8,128)S(1)}, u32[]{:S(2)}, u32[]{:S(2)}) %collective-permute-start.12) | collective-permute-done | bytes 131104 | tf_op jit(solution)/shard_map/ppermute | solution.py:550
  40.6 1.7 %final_kernel.3 = (f32[2,1,4,64,512]{4,3,2,1,0:T(8,128)}, f32[2,1,4,64,512]{4,3,2,1,0:T(8,128)}) custom-call(f32[128,256]{1,0:T(8,128)S(1)} %get-tuple-element.30.refs_2_.refs_0_, f32[128,256]{1,0:T(8,128)S(1)} %collective-permute-done.10.refs_1_, f32[128,256]{1,0:T(8,128)S(1)} %collective-permute-done.11.refs_2_, ...), custom_call_target="tpu_custom_call", output_to_operand_aliasing={{0}: (7, {}), {1}: (8, {})} | custom-call | bytes 5767168 | tf_op jit(solution)/shard_map/final_kernel/pallas_call | solution.py:533
  (6 shorter events, 0.1 us)
Async XLA Ops:
  0.6 1.0 %copy-start.4 = (f32[6,4,64,32]{2,3,1,0:T(8,128)S(1)}, f32[6,4,64,32]{2,3,1,0:T(8,128)}, u32[]{:S(2)}) copy-start(f32[6,4,64,32]{2,3,1,0:T(8,128)} %param.7) | copy-start | bytes 589828
  1.7 10.4 %collective-permute-start.4 = (f32[32,768]{1,0:T(8,128)S(1)}, f32[32,768]{1,0:T(8,128)S(1)}, u32[]{:S(2)}, u32[]{:S(2)}) collective-permute-start(f32[32,768]{1,0:T(8,128)S(1)} %get-tuple-element.22.refs_2_.refs_0_.refs_1_), channel_id=1, source_target_pairs={{0,24},{4,28},{8,16},{12,20},{16,8},{20,12},{24,0},{28,4},{1,25},{... | collective-permute-start | bytes 294920 | tf_op jit(solution)/shard_map/ppermute | solution.py:550
  6.9 7.7 %collective-permute-start.3 = (f32[32,768]{1,0:T(8,128)S(1)}, f32[32,768]{1,0:T(8,128)S(1)}, u32[]{:S(2)}, u32[]{:S(2)}) collective-permute-start(f32[32,768]{1,0:T(8,128)S(1)} %get-tuple-element.21.refs_0_), channel_id=1, source_target_pairs={{0,25},{1,24},{2,27},{3,26},{4,29},{5,28},{6,31},{7,30},{8,17},{9,... | collective-permute-start | bytes 294920 | tf_op jit(solution)/shard_map/ppermute | solution.py:550
  8.0 1.2 %copy-start = (f32[2,1,4,64,512]{4,3,2,1,0:T(8,128)S(1)}, f32[2,1,4,64,512]{4,3,2,1,0:T(8,128)}, u32[]{:S(2)}) copy-start(f32[2,1,4,64,512]{4,3,2,1,0:T(8,128)} %refs_4_.3) | copy-start | bytes 3145732
  9.3 13.7 %collective-permute-start = (f32[4,48,512]{2,1,0:T(8,128)S(1)}, f32[4,48,512]{2,1,0:T(8,128)S(1)}, u32[]{:S(2)}, u32[]{:S(2)}) collective-permute-start(f32[4,48,512]{2,1,0:T(8,128)S(1)} %get-tuple-element.23.refs_1_), channel_id=1, source_target_pairs={{0,2},{1,3},{2,0},{3,1},{4,6},{5,7},{6,4},{7,5},{8,10},{9,11},{10,... | collective-permute-start | bytes 1179656 | tf_op jit(solution)/shard_map/ppermute | solution.py:550
  10.9 6.7 %collective-permute-start.5 = (f32[32,768]{1,0:T(8,128)S(1)}, f32[32,768]{1,0:T(8,128)S(1)}, u32[]{:S(2)}, u32[]{:S(2)}) collective-permute-start(f32[32,768]{1,0:T(8,128)S(1)} %pack_kernel.5), channel_id=1, source_target_pairs={{0,9},{1,8},{2,11},{3,10},{4,13},{5,12},{6,15},{7,14},{8,1},{9,0},... | collective-permute-start | bytes 294920 | tf_op jit(solution)/shard_map/ppermute | solution.py:550
  11.0 11.5 %collective-permute-start.2 = (f32[120,512]{1,0:T(8,128)S(1)}, f32[120,512]{1,0:T(8,128)S(1)}, u32[]{:S(2)}, u32[]{:S(2)}) collective-permute-start(f32[120,512]{1,0:T(8,128)S(1)} %get-tuple-element.25), channel_id=1, source_target_pairs={{0,1},{1,0},{2,3},{3,2},{4,5},{5,4},{6,7},{7,6},{8,9},{9,8},{10,11... | collective-permute-start | bytes 737288 | tf_op jit(solution)/shard_map/ppermute | solution.py:550
  12.2 10.2 %collective-permute-start.7 = (f32[64,768]{1,0:T(8,128)S(1)}, f32[64,768]{1,0:T(8,128)S(1)}, u32[]{:S(2)}, u32[]{:S(2)}) collective-permute-start(f32[64,768]{1,0:T(8,128)S(1)} %pack_kernel.7), channel_id=1, source_target_pairs={{0,8},{4,12},{8,0},{12,4},{16,24},{20,28},{24,16},{28,20},{1,9},{5... | collective-permute-start | bytes 589832 | tf_op jit(solution)/shard_map/ppermute | solution.py:550
  14.5 4.3 %copy-start.1 = (f32[2,1,4,64,512]{4,3,2,1,0:T(8,128)S(1)}, f32[2,1,4,64,512]{4,3,2,1,0:T(8,128)}, u32[]{:S(2)}) copy-start(f32[2,1,4,64,512]{4,3,2,1,0:T(8,128)} %refs_4_.3) | copy-start | bytes 3145732
  14.5 4.3 %copy-start.2 = (bf16[4,256,512]{2,1,0:T(8,128)(2,1)S(1)}, bf16[4,256,512]{2,1,0:T(8,128)(2,1)}, u32[]{:S(2)}) copy-start(bf16[4,256,512]{2,1,0:T(8,128)(2,1)} %constant.4.clone.refs_1_.refs_5_.refs_6_) | copy-start | bytes 3145732
  14.5 7.9 %collective-permute-start.8 = (f32[32,768]{1,0:T(8,128)S(1)}, f32[32,768]{1,0:T(8,128)S(1)}, u32[]{:S(2)}, u32[]{:S(2)}) collective-permute-start(f32[32,768]{1,0:T(8,128)S(1)} %pack_kernel.8), channel_id=1, source_target_pairs={{0,8},{4,12},{8,0},{12,4},{16,24},{20,28},{24,16},{28,20},{1,9},{5... | collective-permute-start | bytes 294920 | tf_op jit(solution)/shard_map/ppermute | solution.py:550
  17.6 5.5 %collective-permute-start.1 = (f32[8,512]{1,0:T(8,128)S(1)}, f32[8,512]{1,0:T(8,128)S(1)}, u32[]{:S(2)}, u32[]{:S(2)}) collective-permute-start(f32[8,512]{1,0:T(8,128)S(1)} %get-tuple-element.24), channel_id=1, source_target_pairs={{0,3},{1,2},{2,1},{3,0},{4,7},{5,6},{6,5},{7,4},{8,11},{9,10},{10,... | collective-permute-start | bytes 49160 | tf_op jit(solution)/shard_map/ppermute | solution.py:550
  18.8 4.2 %copy-start.5 = (bf16[4,2,256,256]{3,2,1,0:T(8,128)(2,1)S(1)}, bf16[4,2,256,256]{3,2,1,0:T(8,128)(2,1)}, u32[]{:S(2)}) copy-start(bf16[4,2,256,256]{3,2,1,0:T(8,128)(2,1)} %constant.5.clone.refs_6_) | copy-start | bytes 3145732
  22.4 2.9 %collective-permute-start.6 = (f32[128,768]{1,0:T(8,128)S(1)}, f32[128,768]{1,0:T(8,128)S(1)}, u32[]{:S(2)}, u32[]{:S(2)}) collective-permute-start(f32[128,768]{1,0:T(8,128)S(1)} %pack_kernel.6.refs_2_), channel_id=1, source_target_pairs={{0,4},{4,0},{8,12},{12,8},{16,20},{20,16},{24,28},{28,24},{1,5},{5... | collective-permute-start | bytes 1179656 | tf_op jit(solution)/shard_map/ppermute | solution.py:550
  22.5 2.9 %collective-permute-start.9 = (f32[128,768]{1,0:T(8,128)S(1)}, f32[128,768]{1,0:T(8,128)S(1)}, u32[]{:S(2)}, u32[]{:S(2)}) collective-permute-start(f32[128,768]{1,0:T(8,128)S(1)} %pack_kernel.9.refs_4_), channel_id=1, source_target_pairs={{0,4},{4,0},{8,12},{12,8},{16,20},{20,16},{24,28},{28,24},{1,5},{5... | collective-permute-start | bytes 1179656 | tf_op jit(solution)/shard_map/ppermute | solution.py:550
  25.9 6.4 %collective-permute-start.13 = (f32[128,256]{1,0:T(8,128)S(1)}, f32[128,256]{1,0:T(8,128)S(1)}, u32[]{:S(2)}, u32[]{:S(2)}) collective-permute-start(f32[128,256]{1,0:T(8,128)S(1)} %get-tuple-element.35), channel_id=1, source_target_pairs={{0,1},{1,0},{2,3},{3,2},{4,5},{5,4},{6,7},{7,6},{8,9},{9,8},{10,11... | collective-permute-start | bytes 393224 | tf_op jit(solution)/shard_map/ppermute | solution.py:550
  26.7 7.2 %collective-permute-start.14 = (f32[128,256]{1,0:T(8,128)S(1)}, f32[128,256]{1,0:T(8,128)S(1)}, u32[]{:S(2)}, u32[]{:S(2)}) collective-permute-start(f32[128,256]{1,0:T(8,128)S(1)} %get-tuple-element.36), channel_id=1, source_target_pairs={{0,2},{1,3},{2,0},{3,1},{4,6},{5,7},{6,4},{7,5},{8,10},{9,11},{10,... | collective-permute-start | bytes 393224 | tf_op jit(solution)/shard_map/ppermute | solution.py:550
  28.0 5.5 %copy-start.3 = (f32[2,1,4,64,512]{4,3,2,1,0:T(8,128)S(1)}, f32[2,1,4,64,512]{4,3,2,1,0:T(8,128)}, u32[]{:S(2)}) copy-start(f32[2,1,4,64,512]{4,3,2,1,0:T(8,128)} %refs_1_.4) | copy-start | bytes 3145732
  28.0 7.9 %collective-permute-start.15 = (f32[128,256]{1,0:T(8,128)S(1)}, f32[128,256]{1,0:T(8,128)S(1)}, u32[]{:S(2)}, u32[]{:S(2)}) collective-permute-start(f32[128,256]{1,0:T(8,128)S(1)} %get-tuple-element.37), channel_id=1, source_target_pairs={{0,3},{1,2},{2,1},{3,0},{4,7},{5,6},{6,5},{7,4},{8,11},{9,10},{10,... | collective-permute-start | bytes 393224 | tf_op jit(solution)/shard_map/ppermute | solution.py:550
  29.9 8.0 %collective-permute-start.10 = (f32[128,256]{1,0:T(8,128)S(1)}, f32[128,256]{1,0:T(8,128)S(1)}, u32[]{:S(2)}, u32[]{:S(2)}) collective-permute-start(f32[128,256]{1,0:T(8,128)S(1)} %get-tuple-element.31), channel_id=1, source_target_pairs={{0,1},{1,0},{2,3},{3,2},{4,5},{5,4},{6,7},{7,6},{8,9},{9,8},{10,11... | collective-permute-start | bytes 393224 | tf_op jit(solution)/shard_map/ppermute | solution.py:550
  30.7 8.4 %collective-permute-start.11 = (f32[128,256]{1,0:T(8,128)S(1)}, f32[128,256]{1,0:T(8,128)S(1)}, u32[]{:S(2)}, u32[]{:S(2)}) collective-permute-start(f32[128,256]{1,0:T(8,128)S(1)} %get-tuple-element.32), channel_id=1, source_target_pairs={{0,2},{1,3},{2,0},{3,1},{4,6},{5,7},{6,4},{7,5},{8,10},{9,11},{10,... | collective-permute-start | bytes 393224 | tf_op jit(solution)/shard_map/ppermute | solution.py:550
  32.3 8.3 %collective-permute-start.12 = (f32[128,256]{1,0:T(8,128)S(1)}, f32[128,256]{1,0:T(8,128)S(1)}, u32[]{:S(2)}, u32[]{:S(2)}) collective-permute-start(f32[128,256]{1,0:T(8,128)S(1)} %get-tuple-element.33), channel_id=1, source_target_pairs={{0,3},{1,2},{2,1},{3,0},{4,7},{5,6},{6,5},{7,4},{8,11},{9,10},{10,... | collective-permute-start | bytes 393224 | tf_op jit(solution)/shard_map/ppermute | solution.py:550

commit v3 on v2

--- a/solution.py
+++ b/solution.py
@@ -177,7 +177,7 @@
 
 PEN = 4
 EXTRA = 8
-NEAR_X = 16
+NEAR_X = 8
 HINT = dict(inverse=10**10, forward=5 * 10**9)
 
 
@@ -591,7 +591,7 @@
     near_rows = exchange(rows_message, "pen", PEN, 2)
     swap_near = across(pack([swap_base], after=[rows_message]), 2)
     came = exchange(swap_message, "pen", PEN, 1)
-    far_rows = exchange(far_message, "pen", PEN, 3)
+    far_rows = exchange(pack([far_message], after=[own_far]), "pen", PEN, 3)
     swap_forward = near(pack([swap_far], HINT["forward"]), 2)
     own_forward = near(pack([own_far, own_base], HINT["forward"]), 2)
     own_parts = call(

time: 42.5 us -> 42.4 us (level)
    pallas_call x14 -> x15, Pallas kernels: 8.19 us -> 8.19 us  [call(): pl.pallas_call(lambda *refs: kernel(*refs[:count], *refs[total:]), out_sh...]
  transfers between devices with their start and end apart: 16 -> 16, of which waited for: 6 -> 7; matrix products, arithmetic and copies ran while one was open for 0% -> 0% of each run, Pallas kernels for 14% -> 14%
where the time goes in v3:
time: 42.4 us; the launch traced here: 42.3 us
  starting transfers between devices  22.9 us (54%)
  Pallas kernels  8.19 us (19%)
  waiting for transfers between devices  8.11 us (19%)
  local copies, waits for them, and re-layouts  2.23 us (5%)
  between operations  0.81 us (2%)
    ppermute x16, starting transfers between devices, exchange(): lax.ppermute(values, axis, [(index, index ^ mask) for index in range(size)])  22.9 us
    pallas_call x15, Pallas kernels, call(): pl.pallas_call(lambda *refs: kernel(*refs[:count], *refs[total:]), out_sh...  8.19 us
    ppermute x16, waiting for transfers between devices, exchange(): lax.ppermute(values, axis, [(index, index ^ mask) for index in range(size)])  8.11 us
    unnamed x12, local copies, waits for them, and re-layouts  2.23 us
  transfers between devices with their start and end apart: 16, of which 7 were waited for; matrix products, arithmetic and copies ran while one was open for 0% of the time, Pallas kernels for 14%

profile of v3, /device:TPU:0, one launch (start us, length us, event | category | flops | bytes accessed | tf_op | source)
XLA Modules:
  0.0 42.3 jit_solution(4328591974575648049)
XLA Ops:
  0.6 0.0 copy-start.4
  0.6 1.0 %copy-done.4 = f32[6,4,64,32]{2,3,1,0:T(8,128)S(1)} copy-done((f32[6,4,64,32]{2,3,1,0:T(8,128)S(1)}, f32[6,4,64,32]{2,3,1,0:T(8,128)}, u32[]{:S(2)}) %copy-start.4) | copy-done | bytes 196632
  1.6 0.1 base_kernel.1
  1.7 5.1 %collective-permute-start.1 = (f32[32,768]{1,0:T(8,128)S(1)}, f32[32,768]{1,0:T(8,128)S(1)}, u32[]{:S(2)}, u32[]{:S(2)}) collective-permute-start(f32[32,768]{1,0:T(8,128)S(1)} %get-tuple-element.22.refs_2_.refs_0_.refs_1_), channel_id=1, source_target_pairs={{0,24},{4,28},{8,16},{12,20},{16,8},{20,12},{24,0},{28,4},{1,25},{... | collective-permute-start | bytes 294920 | tf_op jit(solution)/shard_map/ppermute | solution.py:550
  6.9 1.1 %collective-permute-start.4 = (f32[32,768]{1,0:T(8,128)S(1)}, f32[32,768]{1,0:T(8,128)S(1)}, u32[]{:S(2)}, u32[]{:S(2)}) collective-permute-start(f32[32,768]{1,0:T(8,128)S(1)} %get-tuple-element.21.refs_0_), channel_id=1, source_target_pairs={{0,25},{1,24},{2,27},{3,26},{4,29},{5,28},{6,31},{7,30},{8,17},{9,... | collective-permute-start | bytes 294920 | tf_op jit(solution)/shard_map/ppermute | solution.py:550
  8.0 0.0 copy-start
  8.0 1.2 %copy-done = f32[2,1,4,64,512]{4,3,2,1,0:T(8,128)S(1)} copy-done((f32[2,1,4,64,512]{4,3,2,1,0:T(8,128)S(1)}, f32[2,1,4,64,512]{4,3,2,1,0:T(8,128)}, u32[]{:S(2)}) %copy-start) | copy-done | bytes 1048600
  9.3 1.6 %collective-permute-start = (f32[4,56,512]{2,1,0:T(8,128)S(1)}, f32[4,56,512]{2,1,0:T(8,128)S(1)}, u32[]{:S(2)}, u32[]{:S(2)}) collective-permute-start(f32[4,56,512]{2,1,0:T(8,128)S(1)} %get-tuple-element.23.refs_1_), channel_id=1, source_target_pairs={{0,2},{1,3},{2,0},{3,1},{4,6},{5,7},{6,4},{7,5},{8,10},{9,11},{10,... | collective-permute-start | bytes 1376264 | tf_op jit(solution)/shard_map/ppermute | solution.py:550
  10.9 0.1 collective-permute-start.5
  11.0 1.2 %collective-permute-start.3 = (f32[88,512]{1,0:T(8,128)S(1)}, f32[88,512]{1,0:T(8,128)S(1)}, u32[]{:S(2)}, u32[]{:S(2)}) collective-permute-start(f32[88,512]{1,0:T(8,128)S(1)} %get-tuple-element.25), channel_id=1, source_target_pairs={{0,1},{1,0},{2,3},{3,2},{4,5},{5,4},{6,7},{7,6},{8,9},{9,8},{10,11... | collective-permute-start | bytes 540680 | tf_op jit(solution)/shard_map/ppermute | solution.py:550
  12.2 0.0 collective-permute-done.1.refs_1_.refs_0_
  12.2 2.3 %collective-permute-start.7 = (f32[64,768]{1,0:T(8,128)S(1)}, f32[64,768]{1,0:T(8,128)S(1)}, u32[]{:S(2)}, u32[]{:S(2)}) collective-permute-start(f32[64,768]{1,0:T(8,128)S(1)} %pack_kernel.9), channel_id=1, source_target_pairs={{0,8},{4,12},{8,0},{12,4},{16,24},{20,28},{24,16},{28,20},{1,9},{5... | collective-permute-start | bytes 589832 | tf_op jit(solution)/shard_map/ppermute | solution.py:550
  14.5 0.0 collective-permute-done.4.refs_2_.refs_0_
  14.5 0.0 copy-start.1
  14.5 0.0 copy-start.2
  14.5 3.0 %collective-permute-start.8 = (f32[32,768]{1,0:T(8,128)S(1)}, f32[32,768]{1,0:T(8,128)S(1)}, u32[]{:S(2)}, u32[]{:S(2)}) collective-permute-start(f32[32,768]{1,0:T(8,128)S(1)} %pack_kernel.10), channel_id=1, source_target_pairs={{0,8},{4,12},{8,0},{12,4},{16,24},{20,28},{24,16},{28,20},{1,9},{5... | collective-permute-start | bytes 294920 | tf_op jit(solution)/shard_map/ppermute | solution.py:550
  17.5 0.0 collective-permute-done.5.refs_3_
  17.6 1.2 %collective-permute-start.2 = (f32[8,512]{1,0:T(8,128)S(1)}, f32[8,512]{1,0:T(8,128)S(1)}, u32[]{:S(2)}, u32[]{:S(2)}) collective-permute-start(f32[8,512]{1,0:T(8,128)S(1)} %pack_kernel.6), channel_id=1, source_target_pairs={{0,3},{1,2},{2,1},{3,0},{4,7},{5,6},{6,5},{7,4},{8,11},{9,10},{10,... | collective-permute-start | bytes 49160 | tf_op jit(solution)/shard_map/ppermute | solution.py:550
  18.8 0.0 copy-done.1
  18.8 0.0 copy-done.2
  18.8 0.0 copy-start.5
  18.9 0.8 %own_rows_kernel.1 = (f32[2,6,64,128]{3,2,1,0:T(8,128)S(1)}, f32[2,6,64,128]{3,2,1,0:T(8,128)S(1)}) custom-call(f32[2,1,4,64,512]{4,3,2,1,0:T(8,128)S(1)} %copy-done.1, bf16[4,256,512]{2,1,0:T(8,128)(2,1)S(1)} %copy-done.2, f32[32,768]{1,0:T(8,128)S(1)} %collective-permute-done.4.refs_2_.refs_0_), custom_call_target="tpu_custom_call" | custom-call | bytes 2883584 | tf_op jit(solution)/shard_map/own_rows_kernel/pallas_call | solution.py:533
  19.7 0.4 collective-permute-done.3.refs_2_
  20.1 0.0 collective-permute-start.6
  20.1 2.3 %collective-permute-done.8.refs_1_ = f32[32,768]{1,0:T(8,128)S(1)} collective-permute-done((f32[32,768]{1,0:T(8,128)S(1)}, f32[32,768]{1,0:T(8,128)S(1)}, u32[]{:S(2)}, u32[]{:S(2)}) %collective-permute-start.8) | collective-permute-done | bytes 98336 | tf_op jit(solution)/shard_map/ppermute | solution.py:550
  22.4 0.0 collective-permute-done.7.refs_0_
  22.4 0.1 collective-permute-start.9
  22.5 0.0 collective-permute-done.2.refs_1_
  22.5 0.0 collective-permute-done.refs_0_
  22.5 0.0 copy-done.5
  22.6 2.3 %inverse_kernel.1 = (f32[256,768]{1,0:T(8,128)S(1)}, f32[256,768]{1,0:T(8,128)S(1)}) custom-call(f32[4,56,512]{2,1,0:T(8,128)S(1)} %collective-permute-done.refs_0_, f32[8,512]{1,0:T(8,128)S(1)} %collective-permute-done.2.refs_1_, f32[88,512]{1,0:T(8,128)S(1)} %collective-permute-done.3.refs_2_, f32[2,6,64,128]{3,2,1,0:T(8,128)S(1)} %get-tuple-element.26.refs_3_, ...), custom_call_target="tpu_custom_call" | custom-call | flops 10000000000 | bytes 5111808 | tf_op jit(solution)/shard_map/inverse_kernel/pallas_call | solution.py:533
  24.9 0.0 collective-permute-done.6.refs_3_
  24.9 0.0 collective-permute-done.9.refs_5_
  24.9 0.5 %advection_kernel.3 = (f32[128,256]{1,0:T(8,128)S(1)}, f32[128,256]{1,0:T(8,128)S(1)}, f32[128,256]{1,0:T(8,128)S(1)}, f32[128,256]{1,0:T(8,128)S(1)}) custom-call(f32[256,768]{1,0:T(8,128)S(1)} %get-tuple-element.28.refs_0_, f32[256,768]{1,0:T(8,128)S(1)} %get-tuple-element.29.refs_1_, f32[128,768]{1,0:T(8,128)S(1)} %pack_kernel.8.refs_2_, ...), custom_call_target="tpu_custom_call" | custom-call | bytes 4718592 | tf_op jit(solution)/shard_map/advection_kernel/pallas_call | solution.py:533
  25.4 0.8 %collective-permute-start.13 = (f32[128,256]{1,0:T(8,128)S(1)}, f32[128,256]{1,0:T(8,128)S(1)}, u32[]{:S(2)}, u32[]{:S(2)}) collective-permute-start(f32[128,256]{1,0:T(8,128)S(1)} %get-tuple-element.35), channel_id=1, source_target_pairs={{0,1},{1,0},{2,3},{3,2},{4,5},{5,4},{6,7},{7,6},{8,9},{9,8},{10,11... | collective-permute-start | bytes 393224 | tf_op jit(solution)/shard_map/ppermute | solution.py:550
  26.2 1.3 %collective-permute-start.14 = (f32[128,256]{1,0:T(8,128)S(1)}, f32[128,256]{1,0:T(8,128)S(1)}, u32[]{:S(2)}, u32[]{:S(2)}) collective-permute-start(f32[128,256]{1,0:T(8,128)S(1)} %get-tuple-element.36), channel_id=1, source_target_pairs={{0,2},{1,3},{2,0},{3,1},{4,6},{5,7},{6,4},{7,5},{8,10},{9,11},{10,... | collective-permute-start | bytes 393224 | tf_op jit(solution)/shard_map/ppermute | solution.py:550
  27.5 0.0 copy-start.3
  27.5 1.4 %collective-permute-start.15 = (f32[128,256]{1,0:T(8,128)S(1)}, f32[128,256]{1,0:T(8,128)S(1)}, u32[]{:S(2)}, u32[]{:S(2)}) collective-permute-start(f32[128,256]{1,0:T(8,128)S(1)} %get-tuple-element.37), channel_id=1, source_target_pairs={{0,3},{1,2},{2,1},{3,0},{4,7},{5,6},{6,5},{7,4},{8,11},{9,10},{10,... | collective-permute-start | bytes 393224 | tf_op jit(solution)/shard_map/ppermute | solution.py:550
  28.9 0.5 %advection_kernel.2 = (f32[128,256]{1,0:T(8,128)S(1)}, f32[128,256]{1,0:T(8,128)S(1)}, f32[128,256]{1,0:T(8,128)S(1)}, f32[128,256]{1,0:T(8,128)S(1)}) custom-call(f32[256,768]{1,0:T(8,128)S(1)} %get-tuple-element.28.refs_0_, f32[256,768]{1,0:T(8,128)S(1)} %get-tuple-element.29.refs_1_, f32[128,768]{1,0:T(8,128)S(1)} %pack_kernel.8.refs_2_, ...), custom_call_target="tpu_custom_call" | custom-call | bytes 4718592 | tf_op jit(solution)/shard_map/advection_kernel/pallas_call | solution.py:533
  29.4 0.8 %collective-permute-start.10 = (f32[128,256]{1,0:T(8,128)S(1)}, f32[128,256]{1,0:T(8,128)S(1)}, u32[]{:S(2)}, u32[]{:S(2)}) collective-permute-start(f32[128,256]{1,0:T(8,128)S(1)} %get-tuple-element.31), channel_id=1, source_target_pairs={{0,1},{1,0},{2,3},{3,2},{4,5},{5,4},{6,7},{7,6},{8,9},{9,8},{10,11... | collective-permute-start | bytes 393224 | tf_op jit(solution)/shard_map/ppermute | solution.py:550
  30.2 1.3 %collective-permute-start.11 = (f32[128,256]{1,0:T(8,128)S(1)}, f32[128,256]{1,0:T(8,128)S(1)}, u32[]{:S(2)}, u32[]{:S(2)}) collective-permute-start(f32[128,256]{1,0:T(8,128)S(1)} %get-tuple-element.32), channel_id=1, source_target_pairs={{0,2},{1,3},{2,0},{3,1},{4,6},{5,7},{6,4},{7,5},{8,10},{9,11},{10,... | collective-permute-start | bytes 393224 | tf_op jit(solution)/shard_map/ppermute | solution.py:550
  31.6 0.2 collective-permute-done.13.refs_1_
  31.7 1.5 %collective-permute-start.12 = (f32[128,256]{1,0:T(8,128)S(1)}, f32[128,256]{1,0:T(8,128)S(1)}, u32[]{:S(2)}, u32[]{:S(2)}) collective-permute-start(f32[128,256]{1,0:T(8,128)S(1)} %get-tuple-element.33), channel_id=1, source_target_pairs={{0,3},{1,2},{2,1},{3,0},{4,7},{5,6},{6,5},{7,4},{8,11},{9,10},{10,... | collective-permute-start | bytes 393224 | tf_op jit(solution)/shard_map/ppermute | solution.py:550
  33.2 0.0 copy-done.3
  33.2 0.4 %linear_kernel.1.refs_5_ = f32[2,1,4,64,512]{4,3,2,1,0:T(8,128)S(1)} custom-call(f32[2,1,4,64,512]{4,3,2,1,0:T(8,128)S(1)} %copy-done.1, f32[2,1,4,64,512]{4,3,2,1,0:T(8,128)S(1)} %copy-done.3, f32[128,256]{1,0:T(8,128)S(1)} %get-tuple-element.30.refs_2_.refs_0_), custom_call_target="tpu_custom_call" | custom-call | bytes 3145728 | tf_op jit(solution)/shard_map/linear_kernel/pallas_call | solution.py:533
  33.7 0.0 collective-permute-done.14.refs_2_
  33.7 1.7 %collective-permute-done.15.refs_3_ = f32[128,256]{1,0:T(8,128)S(1)} collective-permute-done((f32[128,256]{1,0:T(8,128)S(1)}, f32[128,256]{1,0:T(8,128)S(1)}, u32[]{:S(2)}, u32[]{:S(2)}) %collective-permute-start.15) | collective-permute-done | bytes 131104 | tf_op jit(solution)/shard_map/ppermute | solution.py:550
  35.3 1.7 %final_kernel.2 = (f32[2,1,4,64,512]{4,3,2,1,0:T(8,128)}, f32[2,1,4,64,512]{4,3,2,1,0:T(8,128)}) custom-call(f32[128,256]{1,0:T(8,128)S(1)} %get-tuple-element.34.refs_0_, f32[128,256]{1,0:T(8,128)S(1)} %collective-permute-done.13.refs_1_, f32[128,256]{1,0:T(8,128)S(1)} %collective-permute-done.14.refs_2_, f32[128,256]{1,0:T(8,128)S(1)} %collective-permute-done.15.refs_3_, ...), custom_call_target="tpu_custom_call" | custom-call | bytes 5767168 | tf_op jit(solution)/shard_map/final_kernel/pallas_call | solution.py:533
  37.0 0.4 collective-permute-done.10.refs_1_
  37.4 0.4 collective-permute-done.11.refs_2_
  37.8 2.8 %collective-permute-done.12.refs_3_ = f32[128,256]{1,0:T(8,128)S(1)} collective-permute-done((f32[128,256]{1,0:T(8,128)S(1)}, f32[128,256]{1,0:T(8,128)S(1)}, u32[]{:S(2)}, u32[]{:S(2)}) %collective-permute-start.12) | collective-permute-done | bytes 131104 | tf_op jit(solution)/shard_map/ppermute | solution.py:550
  40.5 1.7 %final_kernel.3 = (f32[2,1,4,64,512]{4,3,2,1,0:T(8,128)}, f32[2,1,4,64,512]{4,3,2,1,0:T(8,128)}) custom-call(f32[128,256]{1,0:T(8,128)S(1)} %get-tuple-element.30.refs_2_.refs_0_, f32[128,256]{1,0:T(8,128)S(1)} %collective-permute-done.10.refs_1_, f32[128,256]{1,0:T(8,128)S(1)} %collective-permute-done.11.refs_2_, ...), custom_call_target="tpu_custom_call", output_to_operand_aliasing={{0}: (7, {}), {1}: (8, {})} | custom-call | bytes 5767168 | tf_op jit(solution)/shard_map/final_kernel/pallas_call | solution.py:533
  (7 shorter events, 0.1 us)
Async XLA Ops:
  0.6 1.0 %copy-start.4 = (f32[6,4,64,32]{2,3,1,0:T(8,128)S(1)}, f32[6,4,64,32]{2,3,1,0:T(8,128)}, u32[]{:S(2)}) copy-start(f32[6,4,64,32]{2,3,1,0:T(8,128)} %param.7) | copy-start | bytes 589828
  1.7 10.4 %collective-permute-start.1 = (f32[32,768]{1,0:T(8,128)S(1)}, f32[32,768]{1,0:T(8,128)S(1)}, u32[]{:S(2)}, u32[]{:S(2)}) collective-permute-start(f32[32,768]{1,0:T(8,128)S(1)} %get-tuple-element.22.refs_2_.refs_0_.refs_1_), channel_id=1, source_target_pairs={{0,24},{4,28},{8,16},{12,20},{16,8},{20,12},{24,0},{28,4},{1,25},{... | collective-permute-start | bytes 294920 | tf_op jit(solution)/shard_map/ppermute | solution.py:550
  6.9 7.7 %collective-permute-start.4 = (f32[32,768]{1,0:T(8,128)S(1)}, f32[32,768]{1,0:T(8,128)S(1)}, u32[]{:S(2)}, u32[]{:S(2)}) collective-permute-start(f32[32,768]{1,0:T(8,128)S(1)} %get-tuple-element.21.refs_0_), channel_id=1, source_target_pairs={{0,25},{1,24},{2,27},{3,26},{4,29},{5,28},{6,31},{7,30},{8,17},{9,... | collective-permute-start | bytes 294920 | tf_op jit(solution)/shard_map/ppermute | solution.py:550
  8.0 1.2 %copy-start = (f32[2,1,4,64,512]{4,3,2,1,0:T(8,128)S(1)}, f32[2,1,4,64,512]{4,3,2,1,0:T(8,128)}, u32[]{:S(2)}) copy-start(f32[2,1,4,64,512]{4,3,2,1,0:T(8,128)} %refs_4_.3) | copy-start | bytes 3145732
  9.3 13.2 %collective-permute-start = (f32[4,56,512]{2,1,0:T(8,128)S(1)}, f32[4,56,512]{2,1,0:T(8,128)S(1)}, u32[]{:S(2)}, u32[]{:S(2)}) collective-permute-start(f32[4,56,512]{2,1,0:T(8,128)S(1)} %get-tuple-element.23.refs_1_), channel_id=1, source_target_pairs={{0,2},{1,3},{2,0},{3,1},{4,6},{5,7},{6,4},{7,5},{8,10},{9,11},{10,... | collective-permute-start | bytes 1376264 | tf_op jit(solution)/shard_map/ppermute | solution.py:550
  10.9 6.7 %collective-permute-start.5 = (f32[32,768]{1,0:T(8,128)S(1)}, f32[32,768]{1,0:T(8,128)S(1)}, u32[]{:S(2)}, u32[]{:S(2)}) collective-permute-start(f32[32,768]{1,0:T(8,128)S(1)} %pack_kernel.7), channel_id=1, source_target_pairs={{0,9},{1,8},{2,11},{3,10},{4,13},{5,12},{6,15},{7,14},{8,1},{9,0},... | collective-permute-start | bytes 294920 | tf_op jit(solution)/shard_map/ppermute | solution.py:550
  11.0 9.1 %collective-permute-start.3 = (f32[88,512]{1,0:T(8,128)S(1)}, f32[88,512]{1,0:T(8,128)S(1)}, u32[]{:S(2)}, u32[]{:S(2)}) collective-permute-start(f32[88,512]{1,0:T(8,128)S(1)} %get-tuple-element.25), channel_id=1, source_target_pairs={{0,1},{1,0},{2,3},{3,2},{4,5},{5,4},{6,7},{7,6},{8,9},{9,8},{10,11... | collective-permute-start | bytes 540680 | tf_op jit(solution)/shard_map/ppermute | solution.py:550
  12.2 10.2 %collective-permute-start.7 = (f32[64,768]{1,0:T(8,128)S(1)}, f32[64,768]{1,0:T(8,128)S(1)}, u32[]{:S(2)}, u32[]{:S(2)}) collective-permute-start(f32[64,768]{1,0:T(8,128)S(1)} %pack_kernel.9), channel_id=1, source_target_pairs={{0,8},{4,12},{8,0},{12,4},{16,24},{20,28},{24,16},{28,20},{1,9},{5... | collective-permute-start | bytes 589832 | tf_op jit(solution)/shard_map/ppermute | solution.py:550
  14.5 4.3 %copy-start.1 = (f32[2,1,4,64,512]{4,3,2,1,0:T(8,128)S(1)}, f32[2,1,4,64,512]{4,3,2,1,0:T(8,128)}, u32[]{:S(2)}) copy-start(f32[2,1,4,64,512]{4,3,2,1,0:T(8,128)} %refs_4_.3) | copy-start | bytes 3145732
  14.5 4.3 %copy-start.2 = (bf16[4,256,512]{2,1,0:T(8,128)(2,1)S(1)}, bf16[4,256,512]{2,1,0:T(8,128)(2,1)}, u32[]{:S(2)}) copy-start(bf16[4,256,512]{2,1,0:T(8,128)(2,1)} %constant.4.clone.refs_1_.refs_5_.refs_6_) | copy-start | bytes 3145732
  14.5 7.9 %collective-permute-start.8 = (f32[32,768]{1,0:T(8,128)S(1)}, f32[32,768]{1,0:T(8,128)S(1)}, u32[]{:S(2)}, u32[]{:S(2)}) collective-permute-start(f32[32,768]{1,0:T(8,128)S(1)} %pack_kernel.10), channel_id=1, source_target_pairs={{0,8},{4,12},{8,0},{12,4},{16,24},{20,28},{24,16},{28,20},{1,9},{5... | collective-permute-start | bytes 294920 | tf_op jit(solution)/shard_map/ppermute | solution.py:550
  17.6 5.0 %collective-permute-start.2 = (f32[8,512]{1,0:T(8,128)S(1)}, f32[8,512]{1,0:T(8,128)S(1)}, u32[]{:S(2)}, u32[]{:S(2)}) collective-permute-start(f32[8,512]{1,0:T(8,128)S(1)} %pack_kernel.6), channel_id=1, source_target_pairs={{0,3},{1,2},{2,1},{3,0},{4,7},{5,6},{6,5},{7,4},{8,11},{9,10},{10,... | collective-permute-start | bytes 49160 | tf_op jit(solution)/shard_map/ppermute | solution.py:550
  18.8 3.7 %copy-start.5 = (bf16[4,2,256,256]{3,2,1,0:T(8,128)(2,1)S(1)}, bf16[4,2,256,256]{3,2,1,0:T(8,128)(2,1)}, u32[]{:S(2)}) copy-start(bf16[4,2,256,256]{3,2,1,0:T(8,128)(2,1)} %constant.5.clone.refs_6_) | copy-start | bytes 3145732
  20.1 4.8 %collective-permute-start.6 = (f32[128,768]{1,0:T(8,128)S(1)}, f32[128,768]{1,0:T(8,128)S(1)}, u32[]{:S(2)}, u32[]{:S(2)}) collective-permute-start(f32[128,768]{1,0:T(8,128)S(1)} %pack_kernel.8.refs_2_), channel_id=1, source_target_pairs={{0,4},{4,0},{8,12},{12,8},{16,20},{20,16},{24,28},{28,24},{1,5},{5... | collective-permute-start | bytes 1179656 | tf_op jit(solution)/shard_map/ppermute | solution.py:550
  22.4 2.4 %collective-permute-start.9 = (f32[128,768]{1,0:T(8,128)S(1)}, f32[128,768]{1,0:T(8,128)S(1)}, u32[]{:S(2)}, u32[]{:S(2)}) collective-permute-start(f32[128,768]{1,0:T(8,128)S(1)} %pack_kernel.11.refs_4_), channel_id=1, source_target_pairs={{0,4},{4,0},{8,12},{12,8},{16,20},{20,16},{24,28},{28,24},{1,5},{5... | collective-permute-start | bytes 1179656 | tf_op jit(solution)/shard_map/ppermute | solution.py:550
  25.4 6.4 %collective-permute-start.13 = (f32[128,256]{1,0:T(8,128)S(1)}, f32[128,256]{1,0:T(8,128)S(1)}, u32[]{:S(2)}, u32[]{:S(2)}) collective-permute-start(f32[128,256]{1,0:T(8,128)S(1)} %get-tuple-element.35), channel_id=1, source_target_pairs={{0,1},{1,0},{2,3},{3,2},{4,5},{5,4},{6,7},{7,6},{8,9},{9,8},{10,11... | collective-permute-start | bytes 393224 | tf_op jit(solution)/shard_map/ppermute | solution.py:550
  26.2 7.5 %collective-permute-start.14 = (f32[128,256]{1,0:T(8,128)S(1)}, f32[128,256]{1,0:T(8,128)S(1)}, u32[]{:S(2)}, u32[]{:S(2)}) collective-permute-start(f32[128,256]{1,0:T(8,128)S(1)} %get-tuple-element.36), channel_id=1, source_target_pairs={{0,2},{1,3},{2,0},{3,1},{4,6},{5,7},{6,4},{7,5},{8,10},{9,11},{10,... | collective-permute-start | bytes 393224 | tf_op jit(solution)/shard_map/ppermute | solution.py:550
  27.5 5.7 %copy-start.3 = (f32[2,1,4,64,512]{4,3,2,1,0:T(8,128)S(1)}, f32[2,1,4,64,512]{4,3,2,1,0:T(8,128)}, u32[]{:S(2)}) copy-start(f32[2,1,4,64,512]{4,3,2,1,0:T(8,128)} %refs_1_.4) | copy-start | bytes 3145732
  27.5 7.8 %collective-permute-start.15 = (f32[128,256]{1,0:T(8,128)S(1)}, f32[128,256]{1,0:T(8,128)S(1)}, u32[]{:S(2)}, u32[]{:S(2)}) collective-permute-start(f32[128,256]{1,0:T(8,128)S(1)} %get-tuple-element.37), channel_id=1, source_target_pairs={{0,3},{1,2},{2,1},{3,0},{4,7},{5,6},{6,5},{7,4},{8,11},{9,10},{10,... | collective-permute-start | bytes 393224 | tf_op jit(solution)/shard_map/ppermute | solution.py:550
  29.4 8.0 %collective-permute-start.10 = (f32[128,256]{1,0:T(8,128)S(1)}, f32[128,256]{1,0:T(8,128)S(1)}, u32[]{:S(2)}, u32[]{:S(2)}) collective-permute-start(f32[128,256]{1,0:T(8,128)S(1)} %get-tuple-element.31), channel_id=1, source_target_pairs={{0,1},{1,0},{2,3},{3,2},{4,5},{5,4},{6,7},{7,6},{8,9},{9,8},{10,11... | collective-permute-start | bytes 393224 | tf_op jit(solution)/shard_map/ppermute | solution.py:550
  30.2 7.5 %collective-permute-start.11 = (f32[128,256]{1,0:T(8,128)S(1)}, f32[128,256]{1,0:T(8,128)S(1)}, u32[]{:S(2)}, u32[]{:S(2)}) collective-permute-start(f32[128,256]{1,0:T(8,128)S(1)} %get-tuple-element.32), channel_id=1, source_target_pairs={{0,2},{1,3},{2,0},{3,1},{4,6},{5,7},{6,4},{7,5},{8,10},{9,11},{10,... | collective-permute-start | bytes 393224 | tf_op jit(solution)/shard_map/ppermute | solution.py:550
  31.7 8.8 %collective-permute-start.12 = (f32[128,256]{1,0:T(8,128)S(1)}, f32[128,256]{1,0:T(8,128)S(1)}, u32[]{:S(2)}, u32[]{:S(2)}) collective-permute-start(f32[128,256]{1,0:T(8,128)S(1)} %get-tuple-element.33), channel_id=1, source_target_pairs={{0,3},{1,2},{2,1},{3,0},{4,7},{5,6},{6,5},{7,4},{8,11},{9,10},{10,... | collective-permute-start | bytes 393224 | tf_op jit(solution)/shard_map/ppermute | solution.py:550

commit v4 on v3

--- a/solution.py
+++ b/solution.py
@@ -483,12 +483,9 @@
             interleave(gathered[pair + 2 * block, :, first], gathered[pair + 2 * block, :, second])
             for block in range(2)
         ]
-        left = jnp.concatenate(
-            [jnp.concatenate([half[level] for half in halves], axis=1) for level in range(2)], axis=0
-        )
-        product = dot_split(split(left), table)
         for level in (2 * pair, 2 * pair + 1):
-            start = 2 * rows * (level - 2 * pair)
+            left = jnp.concatenate([half[level - 2 * pair] for half in halves], axis=1)
+            product, start = dot_split(split(left), table), 0
             top, bottom = product[start : start + rows], product[start + rows : start + 2 * rows]
             for columns, advect in (
                 (real, top[:, :grid] + bottom[:, grid:]),

time: 42.4 us -> 42.3 us (level)
  no operation moved by 1% of the time
where the time goes in v4:
time: 42.3 us; the launch traced here: 42.1 us
  starting transfers between devices  22.9 us (54%)
  waiting for transfers between devices  8.26 us (20%)
  Pallas kernels  7.88 us (19%)
  local copies, waits for them, and re-layouts  2.23 us (5%)
  between operations  0.81 us (2%)
    ppermute x16, starting transfers between devices, exchange(): lax.ppermute(values, axis, [(index, index ^ mask) for index in range(size)])  22.9 us
    ppermute x16, waiting for transfers between devices, exchange(): lax.ppermute(values, axis, [(index, index ^ mask) for index in range(size)])  8.26 us
    pallas_call x15, Pallas kernels, call(): pl.pallas_call(lambda *refs: kernel(*refs[:count], *refs[total:]), out_sh...  7.88 us
    unnamed x12, local copies, waits for them, and re-layouts  2.23 us
  transfers between devices with their start and end apart: 16, of which 7 were waited for; matrix products, arithmetic and copies ran while one was open for 0% of the time, Pallas kernels for 14%

profile of v4, /device:TPU:0, one launch (start us, length us, event | category | flops | bytes accessed | tf_op | source)
XLA Modules:
  0.0 42.1 jit_solution(5967017093132535571)
XLA Ops:
  0.6 0.0 copy-start.4
  0.6 1.0 %copy-done.4 = f32[6,4,64,32]{2,3,1,0:T(8,128)S(1)} copy-done((f32[6,4,64,32]{2,3,1,0:T(8,128)S(1)}, f32[6,4,64,32]{2,3,1,0:T(8,128)}, u32[]{:S(2)}) %copy-start.4) | copy-done | bytes 196632
  1.6 0.1 base_kernel.1
  1.7 5.1 %collective-permute-start.1 = (f32[32,768]{1,0:T(8,128)S(1)}, f32[32,768]{1,0:T(8,128)S(1)}, u32[]{:S(2)}, u32[]{:S(2)}) collective-permute-start(f32[32,768]{1,0:T(8,128)S(1)} %get-tuple-element.22.refs_2_.refs_0_.refs_1_), channel_id=1, source_target_pairs={{0,24},{4,28},{8,16},{12,20},{16,8},{20,12},{24,0},{28,4},{1,25},{... | collective-permute-start | bytes 294920 | tf_op jit(solution)/shard_map/ppermute | solution.py:547
  6.9 1.1 %collective-permute-start.4 = (f32[32,768]{1,0:T(8,128)S(1)}, f32[32,768]{1,0:T(8,128)S(1)}, u32[]{:S(2)}, u32[]{:S(2)}) collective-permute-start(f32[32,768]{1,0:T(8,128)S(1)} %get-tuple-element.21.refs_0_), channel_id=1, source_target_pairs={{0,25},{1,24},{2,27},{3,26},{4,29},{5,28},{6,31},{7,30},{8,17},{9,... | collective-permute-start | bytes 294920 | tf_op jit(solution)/shard_map/ppermute | solution.py:547
  8.0 0.0 copy-start
  8.0 1.2 %copy-done = f32[2,1,4,64,512]{4,3,2,1,0:T(8,128)S(1)} copy-done((f32[2,1,4,64,512]{4,3,2,1,0:T(8,128)S(1)}, f32[2,1,4,64,512]{4,3,2,1,0:T(8,128)}, u32[]{:S(2)}) %copy-start) | copy-done | bytes 1048600
  9.3 1.6 %collective-permute-start = (f32[4,56,512]{2,1,0:T(8,128)S(1)}, f32[4,56,512]{2,1,0:T(8,128)S(1)}, u32[]{:S(2)}, u32[]{:S(2)}) collective-permute-start(f32[4,56,512]{2,1,0:T(8,128)S(1)} %get-tuple-element.23.refs_1_), channel_id=1, source_target_pairs={{0,2},{1,3},{2,0},{3,1},{4,6},{5,7},{6,4},{7,5},{8,10},{9,11},{10,... | collective-permute-start | bytes 1376264 | tf_op jit(solution)/shard_map/ppermute | solution.py:547
  10.9 0.1 collective-permute-start.5
  11.0 1.2 %collective-permute-start.3 = (f32[88,512]{1,0:T(8,128)S(1)}, f32[88,512]{1,0:T(8,128)S(1)}, u32[]{:S(2)}, u32[]{:S(2)}) collective-permute-start(f32[88,512]{1,0:T(8,128)S(1)} %get-tuple-element.25), channel_id=1, source_target_pairs={{0,1},{1,0},{2,3},{3,2},{4,5},{5,4},{6,7},{7,6},{8,9},{9,8},{10,11... | collective-permute-start | bytes 540680 | tf_op jit(solution)/shard_map/ppermute | solution.py:547
  12.2 0.0 collective-permute-done.1.refs_1_.refs_0_
  12.2 2.3 %collective-permute-start.7 = (f32[64,768]{1,0:T(8,128)S(1)}, f32[64,768]{1,0:T(8,128)S(1)}, u32[]{:S(2)}, u32[]{:S(2)}) collective-permute-start(f32[64,768]{1,0:T(8,128)S(1)} %pack_kernel.9), channel_id=1, source_target_pairs={{0,8},{4,12},{8,0},{12,4},{16,24},{20,28},{24,16},{28,20},{1,9},{5... | collective-permute-start | bytes 589832 | tf_op jit(solution)/shard_map/ppermute | solution.py:547
  14.5 0.0 collective-permute-done.4.refs_2_.refs_0_
  14.5 0.0 copy-start.1
  14.5 0.0 copy-start.2
  14.5 3.0 %collective-permute-start.8 = (f32[32,768]{1,0:T(8,128)S(1)}, f32[32,768]{1,0:T(8,128)S(1)}, u32[]{:S(2)}, u32[]{:S(2)}) collective-permute-start(f32[32,768]{1,0:T(8,128)S(1)} %pack_kernel.10), channel_id=1, source_target_pairs={{0,8},{4,12},{8,0},{12,4},{16,24},{20,28},{24,16},{28,20},{1,9},{5... | collective-permute-start | bytes 294920 | tf_op jit(solution)/shard_map/ppermute | solution.py:547
  17.5 0.0 collective-permute-done.5.refs_3_
  17.6 1.2 %collective-permute-start.2 = (f32[8,512]{1,0:T(8,128)S(1)}, f32[8,512]{1,0:T(8,128)S(1)}, u32[]{:S(2)}, u32[]{:S(2)}) collective-permute-start(f32[8,512]{1,0:T(8,128)S(1)} %pack_kernel.6), channel_id=1, source_target_pairs={{0,3},{1,2},{2,1},{3,0},{4,7},{5,6},{6,5},{7,4},{8,11},{9,10},{10,... | collective-permute-start | bytes 49160 | tf_op jit(solution)/shard_map/ppermute | solution.py:547
  18.8 0.0 copy-done.1
  18.8 0.0 copy-done.2
  18.8 0.0 copy-start.5
  18.9 0.8 %own_rows_kernel.1 = (f32[2,6,64,128]{3,2,1,0:T(8,128)S(1)}, f32[2,6,64,128]{3,2,1,0:T(8,128)S(1)}) custom-call(f32[2,1,4,64,512]{4,3,2,1,0:T(8,128)S(1)} %copy-done.1, bf16[4,256,512]{2,1,0:T(8,128)(2,1)S(1)} %copy-done.2, f32[32,768]{1,0:T(8,128)S(1)} %collective-permute-done.4.refs_2_.refs_0_), custom_call_target="tpu_custom_call" | custom-call | bytes 2883584 | tf_op jit(solution)/shard_map/own_rows_kernel/pallas_call | solution.py:530
  19.7 0.4 collective-permute-done.3.refs_2_
  20.1 0.0 collective-permute-start.6
  20.1 2.3 %collective-permute-done.8.refs_1_ = f32[32,768]{1,0:T(8,128)S(1)} collective-permute-done((f32[32,768]{1,0:T(8,128)S(1)}, f32[32,768]{1,0:T(8,128)S(1)}, u32[]{:S(2)}, u32[]{:S(2)}) %collective-permute-start.8) | collective-permute-done | bytes 98336 | tf_op jit(solution)/shard_map/ppermute | solution.py:547
  22.4 0.0 collective-permute-done.7.refs_0_
  22.4 0.1 collective-permute-start.9
  22.5 0.0 collective-permute-done.2.refs_1_
  22.5 0.0 collective-permute-done.refs_0_
  22.5 0.0 copy-done.5
  22.6 2.3 %inverse_kernel.1 = (f32[256,768]{1,0:T(8,128)S(1)}, f32[256,768]{1,0:T(8,128)S(1)}) custom-call(f32[4,56,512]{2,1,0:T(8,128)S(1)} %collective-permute-done.refs_0_, f32[8,512]{1,0:T(8,128)S(1)} %collective-permute-done.2.refs_1_, f32[88,512]{1,0:T(8,128)S(1)} %collective-permute-done.3.refs_2_, f32[2,6,64,128]{3,2,1,0:T(8,128)S(1)} %get-tuple-element.26.refs_3_, ...), custom_call_target="tpu_custom_call" | custom-call | flops 10000000000 | bytes 5111808 | tf_op jit(solution)/shard_map/inverse_kernel/pallas_call | solution.py:530
  24.9 0.0 collective-permute-done.6.refs_3_
  24.9 0.0 collective-permute-done.9.refs_5_
  24.9 0.5 %advection_kernel.3 = (f32[128,256]{1,0:T(8,128)S(1)}, f32[128,256]{1,0:T(8,128)S(1)}, f32[128,256]{1,0:T(8,128)S(1)}, f32[128,256]{1,0:T(8,128)S(1)}) custom-call(f32[256,768]{1,0:T(8,128)S(1)} %get-tuple-element.28.refs_0_, f32[256,768]{1,0:T(8,128)S(1)} %get-tuple-element.29.refs_1_, f32[128,768]{1,0:T(8,128)S(1)} %pack_kernel.8.refs_2_, ...), custom_call_target="tpu_custom_call" | custom-call | bytes 4718592 | tf_op jit(solution)/shard_map/advection_kernel/pallas_call | solution.py:530
  25.4 0.8 %collective-permute-start.13 = (f32[128,256]{1,0:T(8,128)S(1)}, f32[128,256]{1,0:T(8,128)S(1)}, u32[]{:S(2)}, u32[]{:S(2)}) collective-permute-start(f32[128,256]{1,0:T(8,128)S(1)} %get-tuple-element.35), channel_id=1, source_target_pairs={{0,1},{1,0},{2,3},{3,2},{4,5},{5,4},{6,7},{7,6},{8,9},{9,8},{10,11... | collective-permute-start | bytes 393224 | tf_op jit(solution)/shard_map/ppermute | solution.py:547
  26.2 1.3 %collective-permute-start.14 = (f32[128,256]{1,0:T(8,128)S(1)}, f32[128,256]{1,0:T(8,128)S(1)}, u32[]{:S(2)}, u32[]{:S(2)}) collective-permute-start(f32[128,256]{1,0:T(8,128)S(1)} %get-tuple-element.36), channel_id=1, source_target_pairs={{0,2},{1,3},{2,0},{3,1},{4,6},{5,7},{6,4},{7,5},{8,10},{9,11},{10,... | collective-permute-start | bytes 393224 | tf_op jit(solution)/shard_map/ppermute | solution.py:547
  27.5 0.0 copy-start.3
  27.5 1.4 %collective-permute-start.15 = (f32[128,256]{1,0:T(8,128)S(1)}, f32[128,256]{1,0:T(8,128)S(1)}, u32[]{:S(2)}, u32[]{:S(2)}) collective-permute-start(f32[128,256]{1,0:T(8,128)S(1)} %get-tuple-element.37), channel_id=1, source_target_pairs={{0,3},{1,2},{2,1},{3,0},{4,7},{5,6},{6,5},{7,4},{8,11},{9,10},{10,... | collective-permute-start | bytes 393224 | tf_op jit(solution)/shard_map/ppermute | solution.py:547
  28.9 0.5 %advection_kernel.2 = (f32[128,256]{1,0:T(8,128)S(1)}, f32[128,256]{1,0:T(8,128)S(1)}, f32[128,256]{1,0:T(8,128)S(1)}, f32[128,256]{1,0:T(8,128)S(1)}) custom-call(f32[256,768]{1,0:T(8,128)S(1)} %get-tuple-element.28.refs_0_, f32[256,768]{1,0:T(8,128)S(1)} %get-tuple-element.29.refs_1_, f32[128,768]{1,0:T(8,128)S(1)} %pack_kernel.8.refs_2_, ...), custom_call_target="tpu_custom_call" | custom-call | bytes 4718592 | tf_op jit(solution)/shard_map/advection_kernel/pallas_call | solution.py:530
  29.4 0.8 %collective-permute-start.10 = (f32[128,256]{1,0:T(8,128)S(1)}, f32[128,256]{1,0:T(8,128)S(1)}, u32[]{:S(2)}, u32[]{:S(2)}) collective-permute-start(f32[128,256]{1,0:T(8,128)S(1)} %get-tuple-element.31), channel_id=1, source_target_pairs={{0,1},{1,0},{2,3},{3,2},{4,5},{5,4},{6,7},{7,6},{8,9},{9,8},{10,11... | collective-permute-start | bytes 393224 | tf_op jit(solution)/shard_map/ppermute | solution.py:547
  30.2 1.3 %collective-permute-start.11 = (f32[128,256]{1,0:T(8,128)S(1)}, f32[128,256]{1,0:T(8,128)S(1)}, u32[]{:S(2)}, u32[]{:S(2)}) collective-permute-start(f32[128,256]{1,0:T(8,128)S(1)} %get-tuple-element.32), channel_id=1, source_target_pairs={{0,2},{1,3},{2,0},{3,1},{4,6},{5,7},{6,4},{7,5},{8,10},{9,11},{10,... | collective-permute-start | bytes 393224 | tf_op jit(solution)/shard_map/ppermute | solution.py:547
  31.6 0.2 collective-permute-done.13.refs_1_
  31.7 1.5 %collective-permute-start.12 = (f32[128,256]{1,0:T(8,128)S(1)}, f32[128,256]{1,0:T(8,128)S(1)}, u32[]{:S(2)}, u32[]{:S(2)}) collective-permute-start(f32[128,256]{1,0:T(8,128)S(1)} %get-tuple-element.33), channel_id=1, source_target_pairs={{0,3},{1,2},{2,1},{3,0},{4,7},{5,6},{6,5},{7,4},{8,11},{9,10},{10,... | collective-permute-start | bytes 393224 | tf_op jit(solution)/shard_map/ppermute | solution.py:547
  33.2 0.0 copy-done.3
  33.2 0.4 %linear_kernel.1.refs_5_ = f32[2,1,4,64,512]{4,3,2,1,0:T(8,128)S(1)} custom-call(f32[2,1,4,64,512]{4,3,2,1,0:T(8,128)S(1)} %copy-done.1, f32[2,1,4,64,512]{4,3,2,1,0:T(8,128)S(1)} %copy-done.3, f32[128,256]{1,0:T(8,128)S(1)} %get-tuple-element.30.refs_2_.refs_0_), custom_call_target="tpu_custom_call" | custom-call | bytes 3145728 | tf_op jit(solution)/shard_map/linear_kernel/pallas_call | solution.py:530
  33.7 0.0 collective-permute-done.14.refs_2_
  33.7 1.7 %collective-permute-done.15.refs_3_ = f32[128,256]{1,0:T(8,128)S(1)} collective-permute-done((f32[128,256]{1,0:T(8,128)S(1)}, f32[128,256]{1,0:T(8,128)S(1)}, u32[]{:S(2)}, u32[]{:S(2)}) %collective-permute-start.15) | collective-permute-done | bytes 131104 | tf_op jit(solution)/shard_map/ppermute | solution.py:547
  35.3 1.5 %final_kernel.2 = (f32[2,1,4,64,512]{4,3,2,1,0:T(8,128)}, f32[2,1,4,64,512]{4,3,2,1,0:T(8,128)}) custom-call(f32[128,256]{1,0:T(8,128)S(1)} %get-tuple-element.34.refs_0_, f32[128,256]{1,0:T(8,128)S(1)} %collective-permute-done.13.refs_1_, f32[128,256]{1,0:T(8,128)S(1)} %collective-permute-done.14.refs_2_, f32[128,256]{1,0:T(8,128)S(1)} %collective-permute-done.15.refs_3_, ...), custom_call_target="tpu_custom_call" | custom-call | bytes 5767168 | tf_op jit(solution)/shard_map/final_kernel/pallas_call | solution.py:530
  36.9 0.5 %collective-permute-done.10.refs_1_ = f32[128,256]{1,0:T(8,128)S(1)} collective-permute-done((f32[128,256]{1,0:T(8,128)S(1)}, f32[128,256]{1,0:T(8,128)S(1)}, u32[]{:S(2)}, u32[]{:S(2)}) %collective-permute-start.10) | collective-permute-done | bytes 131104 | tf_op jit(solution)/shard_map/ppermute | solution.py:547
  37.4 0.4 collective-permute-done.11.refs_2_
  37.8 2.8 %collective-permute-done.12.refs_3_ = f32[128,256]{1,0:T(8,128)S(1)} collective-permute-done((f32[128,256]{1,0:T(8,128)S(1)}, f32[128,256]{1,0:T(8,128)S(1)}, u32[]{:S(2)}, u32[]{:S(2)}) %collective-permute-start.12) | collective-permute-done | bytes 131104 | tf_op jit(solution)/shard_map/ppermute | solution.py:547
  40.5 1.5 %final_kernel.3 = (f32[2,1,4,64,512]{4,3,2,1,0:T(8,128)}, f32[2,1,4,64,512]{4,3,2,1,0:T(8,128)}) custom-call(f32[128,256]{1,0:T(8,128)S(1)} %get-tuple-element.30.refs_2_.refs_0_, f32[128,256]{1,0:T(8,128)S(1)} %collective-permute-done.10.refs_1_, f32[128,256]{1,0:T(8,128)S(1)} %collective-permute-done.11.refs_2_, ...), custom_call_target="tpu_custom_call", output_to_operand_aliasing={{0}: (7, {}), {1}: (8, {})} | custom-call | bytes 5767168 | tf_op jit(solution)/shard_map/final_kernel/pallas_call | solution.py:530
  (7 shorter events, 0.1 us)
Async XLA Ops:
  0.6 1.0 %copy-start.4 = (f32[6,4,64,32]{2,3,1,0:T(8,128)S(1)}, f32[6,4,64,32]{2,3,1,0:T(8,128)}, u32[]{:S(2)}) copy-start(f32[6,4,64,32]{2,3,1,0:T(8,128)} %param.7) | copy-start | bytes 589828
  1.7 10.4 %collective-permute-start.1 = (f32[32,768]{1,0:T(8,128)S(1)}, f32[32,768]{1,0:T(8,128)S(1)}, u32[]{:S(2)}, u32[]{:S(2)}) collective-permute-start(f32[32,768]{1,0:T(8,128)S(1)} %get-tuple-element.22.refs_2_.refs_0_.refs_1_), channel_id=1, source_target_pairs={{0,24},{4,28},{8,16},{12,20},{16,8},{20,12},{24,0},{28,4},{1,25},{... | collective-permute-start | bytes 294920 | tf_op jit(solution)/shard_map/ppermute | solution.py:547
  6.9 7.7 %collective-permute-start.4 = (f32[32,768]{1,0:T(8,128)S(1)}, f32[32,768]{1,0:T(8,128)S(1)}, u32[]{:S(2)}, u32[]{:S(2)}) collective-permute-start(f32[32,768]{1,0:T(8,128)S(1)} %get-tuple-element.21.refs_0_), channel_id=1, source_target_pairs={{0,25},{1,24},{2,27},{3,26},{4,29},{5,28},{6,31},{7,30},{8,17},{9,... | collective-permute-start | bytes 294920 | tf_op jit(solution)/shard_map/ppermute | solution.py:547
  8.0 1.2 %copy-start = (f32[2,1,4,64,512]{4,3,2,1,0:T(8,128)S(1)}, f32[2,1,4,64,512]{4,3,2,1,0:T(8,128)}, u32[]{:S(2)}) copy-start(f32[2,1,4,64,512]{4,3,2,1,0:T(8,128)} %refs_4_.3) | copy-start | bytes 3145732
  9.3 13.2 %collective-permute-start = (f32[4,56,512]{2,1,0:T(8,128)S(1)}, f32[4,56,512]{2,1,0:T(8,128)S(1)}, u32[]{:S(2)}, u32[]{:S(2)}) collective-permute-start(f32[4,56,512]{2,1,0:T(8,128)S(1)} %get-tuple-element.23.refs_1_), channel_id=1, source_target_pairs={{0,2},{1,3},{2,0},{3,1},{4,6},{5,7},{6,4},{7,5},{8,10},{9,11},{10,... | collective-permute-start | bytes 1376264 | tf_op jit(solution)/shard_map/ppermute | solution.py:547
  10.9 6.7 %collective-permute-start.5 = (f32[32,768]{1,0:T(8,128)S(1)}, f32[32,768]{1,0:T(8,128)S(1)}, u32[]{:S(2)}, u32[]{:S(2)}) collective-permute-start(f32[32,768]{1,0:T(8,128)S(1)} %pack_kernel.7), channel_id=1, source_target_pairs={{0,9},{1,8},{2,11},{3,10},{4,13},{5,12},{6,15},{7,14},{8,1},{9,0},... | collective-permute-start | bytes 294920 | tf_op jit(solution)/shard_map/ppermute | solution.py:547
  11.0 9.1 %collective-permute-start.3 = (f32[88,512]{1,0:T(8,128)S(1)}, f32[88,512]{1,0:T(8,128)S(1)}, u32[]{:S(2)}, u32[]{:S(2)}) collective-permute-start(f32[88,512]{1,0:T(8,128)S(1)} %get-tuple-element.25), channel_id=1, source_target_pairs={{0,1},{1,0},{2,3},{3,2},{4,5},{5,4},{6,7},{7,6},{8,9},{9,8},{10,11... | collective-permute-start | bytes 540680 | tf_op jit(solution)/shard_map/ppermute | solution.py:547
  12.2 10.2 %collective-permute-start.7 = (f32[64,768]{1,0:T(8,128)S(1)}, f32[64,768]{1,0:T(8,128)S(1)}, u32[]{:S(2)}, u32[]{:S(2)}) collective-permute-start(f32[64,768]{1,0:T(8,128)S(1)} %pack_kernel.9), channel_id=1, source_target_pairs={{0,8},{4,12},{8,0},{12,4},{16,24},{20,28},{24,16},{28,20},{1,9},{5... | collective-permute-start | bytes 589832 | tf_op jit(solution)/shard_map/ppermute | solution.py:547
  14.5 4.3 %copy-start.1 = (f32[2,1,4,64,512]{4,3,2,1,0:T(8,128)S(1)}, f32[2,1,4,64,512]{4,3,2,1,0:T(8,128)}, u32[]{:S(2)}) copy-start(f32[2,1,4,64,512]{4,3,2,1,0:T(8,128)} %refs_4_.3) | copy-start | bytes 3145732
  14.5 4.3 %copy-start.2 = (bf16[4,256,512]{2,1,0:T(8,128)(2,1)S(1)}, bf16[4,256,512]{2,1,0:T(8,128)(2,1)}, u32[]{:S(2)}) copy-start(bf16[4,256,512]{2,1,0:T(8,128)(2,1)} %constant.4.clone.refs_1_.refs_5_.refs_6_) | copy-start | bytes 3145732
  14.5 7.9 %collective-permute-start.8 = (f32[32,768]{1,0:T(8,128)S(1)}, f32[32,768]{1,0:T(8,128)S(1)}, u32[]{:S(2)}, u32[]{:S(2)}) collective-permute-start(f32[32,768]{1,0:T(8,128)S(1)} %pack_kernel.10), channel_id=1, source_target_pairs={{0,8},{4,12},{8,0},{12,4},{16,24},{20,28},{24,16},{28,20},{1,9},{5... | collective-permute-start | bytes 294920 | tf_op jit(solution)/shard_map/ppermute | solution.py:547
  17.6 5.0 %collective-permute-start.2 = (f32[8,512]{1,0:T(8,128)S(1)}, f32[8,512]{1,0:T(8,128)S(1)}, u32[]{:S(2)}, u32[]{:S(2)}) collective-permute-start(f32[8,512]{1,0:T(8,128)S(1)} %pack_kernel.6), channel_id=1, source_target_pairs={{0,3},{1,2},{2,1},{3,0},{4,7},{5,6},{6,5},{7,4},{8,11},{9,10},{10,... | collective-permute-start | bytes 49160 | tf_op jit(solution)/shard_map/ppermute | solution.py:547
  18.8 3.7 %copy-start.5 = (bf16[4,2,256,256]{3,2,1,0:T(8,128)(2,1)S(1)}, bf16[4,2,256,256]{3,2,1,0:T(8,128)(2,1)}, u32[]{:S(2)}) copy-start(bf16[4,2,256,256]{3,2,1,0:T(8,128)(2,1)} %constant.5.clone.refs_6_) | copy-start | bytes 3145732
  20.1 4.8 %collective-permute-start.6 = (f32[128,768]{1,0:T(8,128)S(1)}, f32[128,768]{1,0:T(8,128)S(1)}, u32[]{:S(2)}, u32[]{:S(2)}) collective-permute-start(f32[128,768]{1,0:T(8,128)S(1)} %pack_kernel.8.refs_2_), channel_id=1, source_target_pairs={{0,4},{4,0},{8,12},{12,8},{16,20},{20,16},{24,28},{28,24},{1,5},{5... | collective-permute-start | bytes 1179656 | tf_op jit(solution)/shard_map/ppermute | solution.py:547
  22.4 2.4 %collective-permute-start.9 = (f32[128,768]{1,0:T(8,128)S(1)}, f32[128,768]{1,0:T(8,128)S(1)}, u32[]{:S(2)}, u32[]{:S(2)}) collective-permute-start(f32[128,768]{1,0:T(8,128)S(1)} %pack_kernel.11.refs_4_), channel_id=1, source_target_pairs={{0,4},{4,0},{8,12},{12,8},{16,20},{20,16},{24,28},{28,24},{1,5},{5... | collective-permute-start | bytes 1179656 | tf_op jit(solution)/shard_map/ppermute | solution.py:547
  25.4 6.4 %collective-permute-start.13 = (f32[128,256]{1,0:T(8,128)S(1)}, f32[128,256]{1,0:T(8,128)S(1)}, u32[]{:S(2)}, u32[]{:S(2)}) collective-permute-start(f32[128,256]{1,0:T(8,128)S(1)} %get-tuple-element.35), channel_id=1, source_target_pairs={{0,1},{1,0},{2,3},{3,2},{4,5},{5,4},{6,7},{7,6},{8,9},{9,8},{10,11... | collective-permute-start | bytes 393224 | tf_op jit(solution)/shard_map/ppermute | solution.py:547
  26.2 7.5 %collective-permute-start.14 = (f32[128,256]{1,0:T(8,128)S(1)}, f32[128,256]{1,0:T(8,128)S(1)}, u32[]{:S(2)}, u32[]{:S(2)}) collective-permute-start(f32[128,256]{1,0:T(8,128)S(1)} %get-tuple-element.36), channel_id=1, source_target_pairs={{0,2},{1,3},{2,0},{3,1},{4,6},{5,7},{6,4},{7,5},{8,10},{9,11},{10,... | collective-permute-start | bytes 393224 | tf_op jit(solution)/shard_map/ppermute | solution.py:547
  27.5 5.7 %copy-start.3 = (f32[2,1,4,64,512]{4,3,2,1,0:T(8,128)S(1)}, f32[2,1,4,64,512]{4,3,2,1,0:T(8,128)}, u32[]{:S(2)}) copy-start(f32[2,1,4,64,512]{4,3,2,1,0:T(8,128)} %refs_1_.4) | copy-start | bytes 3145732
  27.5 7.8 %collective-permute-start.15 = (f32[128,256]{1,0:T(8,128)S(1)}, f32[128,256]{1,0:T(8,128)S(1)}, u32[]{:S(2)}, u32[]{:S(2)}) collective-permute-start(f32[128,256]{1,0:T(8,128)S(1)} %get-tuple-element.37), channel_id=1, source_target_pairs={{0,3},{1,2},{2,1},{3,0},{4,7},{5,6},{6,5},{7,4},{8,11},{9,10},{10,... | collective-permute-start | bytes 393224 | tf_op jit(solution)/shard_map/ppermute | solution.py:547
  29.4 8.0 %collective-permute-start.10 = (f32[128,256]{1,0:T(8,128)S(1)}, f32[128,256]{1,0:T(8,128)S(1)}, u32[]{:S(2)}, u32[]{:S(2)}) collective-permute-start(f32[128,256]{1,0:T(8,128)S(1)} %get-tuple-element.31), channel_id=1, source_target_pairs={{0,1},{1,0},{2,3},{3,2},{4,5},{5,4},{6,7},{7,6},{8,9},{9,8},{10,11... | collective-permute-start | bytes 393224 | tf_op jit(solution)/shard_map/ppermute | solution.py:547
  30.2 7.5 %collective-permute-start.11 = (f32[128,256]{1,0:T(8,128)S(1)}, f32[128,256]{1,0:T(8,128)S(1)}, u32[]{:S(2)}, u32[]{:S(2)}) collective-permute-start(f32[128,256]{1,0:T(8,128)S(1)} %get-tuple-element.32), channel_id=1, source_target_pairs={{0,2},{1,3},{2,0},{3,1},{4,6},{5,7},{6,4},{7,5},{8,10},{9,11},{10,... | collective-permute-start | bytes 393224 | tf_op jit(solution)/shard_map/ppermute | solution.py:547
  31.7 8.8 %collective-permute-start.12 = (f32[128,256]{1,0:T(8,128)S(1)}, f32[128,256]{1,0:T(8,128)S(1)}, u32[]{:S(2)}, u32[]{:S(2)}) collective-permute-start(f32[128,256]{1,0:T(8,128)S(1)} %get-tuple-element.33), channel_id=1, source_target_pairs={{0,3},{1,2},{2,1},{3,0},{4,7},{5,6},{6,5},{7,4},{8,11},{9,10},{10,... | collective-permute-start | bytes 393224 | tf_op jit(solution)/shard_map/ppermute | solution.py:547
